TPU v7x, 32 devices: a whole 2x2x4 slice. The times are simulated.
32 devices in a mesh: groups: 2 (over x), dom: 8 (over z, y), slab: 2 (over core).
Axes of the slice: x: 2, y: 2, z: 4, core: 2. Of those that a mesh axis runs over, the one named last changes fastest.
Arguments:
- particles: float32 [16, 64, 128, 128], P(('groups', 'dom'), 'slab'), parts along dimension 0, may hold values from -3 to 3
- state_zero: bfloat16 [16, 64, 128, 128], P(('groups', 'dom'), 'slab'), parts along dimension 0, may hold values from -6 to 6
- state_one: bfloat16 [16, 64, 128, 128], P(('groups', 'dom'), 'slab'), parts along dimension 0, may hold values from -6 to 6
- source: float32 [128, 128, 128], P(('groups', 'slab')), parts along dimension 0, may hold values from -6 to 6
- observed: float32 [128, 128, 128], P(('groups', 'slab')), parts along dimension 0, may hold values from -6 to 6
- absorb: float32 [128, 128, 128], P(('groups', 'slab')), parts along dimension 0, may hold values from 0.5 to 2
- kernel: float32 [16, 8], P('groups'), parts along dimension 0, may hold values from 0.05 to 1
- inv_width: float32 [2], P('groups'), parts along dimension 0, may hold values from 0.5 to 2
Outputs:
- step_dir: float32 [16, 64, 128, 128], P(('groups', 'dom'), 'slab'), parts along dimension 0
There are 2 independent parts, one for each index of `groups`. A program takes and returns all parts, laid end to end along the dimension named above; each array names one. Nothing has to cross between parts.
All inputs are finite; a program needn't handle non-finite values.
Results may differ from a plain program's by a relative error of at most 0.0021.
Values may be sent and summed in bfloat16 or wider, within the bound.
No kernel may reach another device: no remote copies, remote signals or barrier semaphores. Data moves between devices by JAX's collectives and lax.ppermute only.
A program may use at most 64 MiB of HBM per device.

v0:
```python
import jax
import jax.numpy as jnp
from jax import lax
from jax.sharding import PartitionSpec as P

misfit_weight = 8.0


def extended_2(value, sides, width):
    for axis, dim in sides:
        size, length = (lax.axis_size(axis), value.shape[dim])
        up = [(i, (i + 1) % size) for i in range(size - 1)]
        down = [(j, i) for i, j in up]
        last = lax.slice_in_dim(value, length - width, length, axis=dim)
        first = lax.slice_in_dim(value, 0, width, axis=dim)
        before = lax.ppermute(last, axis, up)
        after = lax.ppermute(first, axis, down)
        value = jnp.concatenate([before, value, after], axis=dim)
    return value


def rim_neighbours(extended):
    center = extended[..., 1:-1, :, :]
    lead = [(0, 0)] * (center.ndim - 2)
    padded = jnp.pad(center, lead + [(1, 1), (1, 1)])
    total = extended[..., 2:, :, :] + extended[..., :-2, :, :]
    total = total + padded[..., 2:, 1:-1] + padded[..., :-2, 1:-1]
    total = total + padded[..., 1:-1, 2:] + padded[..., 1:-1, :-2]
    return total


def shards(particles, state_zero, state_one, source, observed, absorb, kernel, inv_width):
    repulsion = inv_width[0]
    part_count = particles.shape[0]
    count = kernel.shape[0]
    stacked = jnp.stack([state_zero, state_one])
    extended = extended_2(stacked, (("slab", 2),), 1)
    near_both = rim_neighbours(extended.astype(jnp.float32))
    near_zero = near_both[0]
    near_one = near_both[1]
    conduct = jnp.exp(particles)
    denominator = 6.0 * conduct + absorb
    state_two = (source + conduct * near_one) / denominator
    adj_two = misfit_weight * (state_two - observed)
    weighted = conduct / denominator * adj_two
    weighted_ext = extended_2(weighted, (("slab", 1),), 1)
    adj_one = rim_neighbours(weighted_ext)
    gradient = -particles - conduct * (
        adj_two * (absorb * near_one - 6.0 * source) + adj_one * (absorb * near_zero - 6.0 * source)
    ) / (denominator * denominator)
    carried = (gradient - repulsion * particles).astype(jnp.bfloat16).reshape(part_count, -1)
    weights = kernel.astype(jnp.bfloat16)
    first_own = lax.axis_index("dom") * part_count
    cell_view = lax.all_to_all(carried, "dom", split_axis=1, concat_axis=0, tiled=True)
    mixed_cells = jnp.dot(weights.T, cell_view, preferred_element_type=jnp.float32)
    mixed = lax.all_to_all(mixed_cells, "dom", split_axis=0, concat_axis=1, tiled=True)
    column_sums = jnp.sum(lax.dynamic_slice_in_dim(kernel, first_own, part_count, 1), axis=0)
    result = (
        mixed.reshape(particles.shape) + repulsion * particles * column_sums[:, None, None, None]
    )
    return result / count


def solution(mesh):
    return jax.shard_map(
        shards,
        mesh=mesh,
        in_specs=(
            P(("groups", "dom"), "slab", None, None),
            P(("groups", "dom"), "slab", None, None),
            P(("groups", "dom"), "slab", None, None),
            P(("groups", "slab"), None, None),
            P(("groups", "slab"), None, None),
            P(("groups", "slab"), None, None),
            P("groups", None),
            P("groups"),
        ),
        out_specs=P(("groups", "dom"), "slab", None, None),
        check_vma=False,
    )
```

profile of v0, /device:TPU:0, one launch (start us, length us, event | category | flops | bytes accessed | tf_op | source)
XLA Modules:
  0.0 133.6 jit_solution(2233785253483829539)
XLA Ops:
  0.0 0.0 copy-start.5
  0.0 0.0 copy-start.4
  0.0 1.0 pad_maximum_fusion.3
  1.0 2.4 %collective-permute-start = (bf16[2,1,1,128,128]{4,3,2,1,0:T(8,128)(2,1)S(1)}, bf16[2,1,1,128,128]{4,3,2,1,0:T(8,128)(2,1)S(1)}, u32[]{:S(2)}, u32[]{:S(2)}) collective-permute-start(bf16[2,1,1,128,128]{4,3,2,1,0:T(8,128)(2,1)S(1)} %get-tuple-element.7), channel_id=1, source_target_pairs={{0,1},{2,3},{4,5},{6,7},{8,9},{10,11},{12,13},{14,15},{16,17},{18,... | collective-permute-start | bytes 196616 | tf_op jit(solution)/shard_map/ppermute | solution.py:16
  3.3 1.3 collective-permute-start.1
  4.6 0.0 collective-permute-done
  4.7 1.8 %collective-permute-done.1 = bf16[2,1,1,128,128]{4,3,2,1,0:T(8,128)(2,1)S(1)} collective-permute-done((bf16[2,1,1,128,128]{4,3,2,1,0:T(8,128)(2,1)S(1)}, bf16[2,1,1,128,128]{4,3,2,1,0:T(8,128)(2,1)S(1)}, u32[]{:S(2)}, u32[]{:S(2)}) %collective-permute-start.1) | collective-permute-done | bytes 65568 | tf_op jit(solution)/shard_map/ppermute | solution.py:17
  6.5 0.0 copy-done.5
  6.5 0.0 copy-done.4
  6.5 0.4 maximum_convert_fusion
  6.9 0.5 slice.80
  7.4 0.0 copy-start
  7.4 0.0 copy-start.1
  7.5 0.0 copy-start.2
  7.5 0.0 copy-start.3
  7.5 2.8 %fusion.3 = f32[2,1,32,128,128]{4,3,2,1,0:T(8,128)S(1)} fusion(f32[2,1,32,128,128]{4,3,2,1,0:T(8,128)S(1)} %slice.80, f32[2,1,34,128,128]{4,3,2,1,0:T(8,128)S(1)} %maximum_convert_fusion), kind=kLoop, calls=%fused_computation.12 | loop fusion | flops 5242880 | bytes 16777216 | tf_op jit(solution)/shard_map/add | solution.py:28
  10.3 0.0 copy-done
  10.3 0.0 copy-done.1
  10.3 0.0 copy-done.2
  10.3 0.6 copy-done.3
  10.9 1.2 divide_multiply_fusion
  12.1 1.3 collective-permute-start.2
  13.4 3.2 %collective-permute-start.3 = (f32[1,1,128,128]{3,2,1,0:T(8,128)S(1)}, f32[1,1,128,128]{3,2,1,0:T(8,128)S(1)}, u32[]{:S(2)}, u32[]{:S(2)}) collective-permute-start(f32[1,1,128,128]{3,2,1,0:T(8,128)S(1)} %get-tuple-element.6), channel_id=1, source_target_pairs={{0,1},{2,3},{4,5},{6,7},{8,9},{10,11},{12,13},{14,15},{16,17},{18,... | collective-permute-start | bytes 196616 | tf_op jit(solution)/shard_map/ppermute | solution.py:16
  17.3 0.0 collective-permute-done.2
  17.3 0.0 collective-permute-done.3
  17.3 3.4 %fusion.22 = bf16[1,32,128,128]{3,2,1,0:T(8,128)(2,1)S(1)} fusion(f32[32,128,128]{2,1,0:T(8,128)S(1)} %copy-done.1, f32[2,1,32,128,128]{4,3,2,1,0:T(8,128)S(1)} %fusion.3, f32[1,32,128,128]{3,2,1,0:T(8,128)S(1)} %divide_multiply_fusion, f32[1,1,128,128]{3,2,1,0:T(8,128)S(1)} %collective-permute-done.3, f32[1,1,128,128]{3,2,1,0:T(8,128)S(1)} %collective-permute-done.2, ...), kind=kLoop, calls=%fused_computation.43 | loop fusion | flops 15728640 | bytes 15859716 | tf_op jit(solution)/shard_map/convert_element_type | solution.py:51
  20.7 3.1 %all_to_all.27 = bf16[1,8,65536]{2,0,1:T(2,128)(2,1)} reshape(bf16[1,32,128,128]{3,2,1,0:T(8,128)(2,1)S(1)} %fusion.22) | data formatting | bytes 2097152 | tf_op jit(solution)/shard_map/all_to_all | solution.py:54
  23.8 0.6 broadcast.22
  24.4 8.4 %reduce.1 = bf16[8,65536]{1,0:T(8,128)(2,1)S(1)} reduce(bf16[8,1,65536]{2,1,0:T(2,128)(2,1)} %bitcast.95, bf16[]{:T(256)} %broadcast.22), dimensions={1}, to_apply=%bitcast.91.reduce_sub_computation | reduce | bytes 2097154
  32.8 1.9 %reshape.70 = bf16[8,2,32768]{2,1,0:T(2,128)(2,1)} reshape(bf16[8,65536]{1,0:T(8,128)(2,1)S(1)} %reduce.1) | data formatting | bytes 2097152
  34.6 32.9 %all_to_all.30 = bf16[8,2,32768]{2,1,0:T(2,128)(2,1)S(1)} all-to-all(bf16[8,2,32768]{2,1,0:T(2,128)(2,1)} %reshape.70), channel_id=1, replica_groups=mesh['groups'=2,'dom'=8,'slab'=2] {'dom'}, dimensions={0} | all-to-all | bytes 2097152 | tf_op jit(solution)/shard_map/all_to_all | solution.py:54
  67.5 0.0 copy-start.6
  67.5 3.4 %reshape.71 = bf16[8,1,65536]{2,1,0:T(2,128)(2,1)} reshape(bf16[8,2,32768]{2,1,0:T(2,128)(2,1)S(1)} %all_to_all.30) | data formatting | bytes 2097152
  70.9 0.0 copy-done.6
  70.9 2.8 %convolution_bitcast_fusion = f32[8,1,65536]{2,0,1:T(8,128)S(1)} fusion(bf16[1,8,65536]{2,0,1:T(2,128)(2,1)} %bitcast.96, f32[8,8]{1,0:T(8,128)S(1)} %copy-done.6), kind=kOutput, calls=%fused_computation | convolution fusion | flops 8388672 | bytes 3145984 | tf_op jit(solution)/shard_map/dot_general | solution.py:55
  73.8 3.5 %copy.11 = f32[8,1,65536]{2,1,0:T(1,128)} copy(f32[8,1,65536]{2,0,1:T(8,128)S(1)} %convolution_bitcast_fusion) | data formatting | bytes 4194304 | tf_op jit(solution)/shard_map/all_to_all | solution.py:56
  77.3 4.3 %all-to-all-start.1 = ((f32[8,1,65536]{2,1,0:T(1,128)}), f32[8,1,65536]{2,1,0:T(1,128)}, u32[]{:S(2)}, u32[]{:S(2)}) async-start(f32[8,1,65536]{2,1,0:T(1,128)} %copy.11), calls=%async_computation.1 | async-start | bytes 4194304 | tf_op jit(solution)/shard_map/all_to_all | solution.py:56
  81.6 0.7 dynamic-slice_reduce_fusion
  82.4 47.2 %all-to-all-done.1 = f32[8,1,65536]{2,1,0:T(1,128)} async-done(((f32[8,1,65536]{2,1,0:T(1,128)}), f32[8,1,65536]{2,1,0:T(1,128)}, u32[]{:S(2)}, u32[]{:S(2)}) %all-to-all-start.1) | async-done | bytes 2097184 | tf_op jit(solution)/shard_map/all_to_all | solution.py:56
  129.5 4.1 %add_multiply_fusion = f32[1,32,128,128]{3,2,1,0:T(8,128)} fusion(f32[1,32,128,128]{3,2,1,0:T(8,128)} %bitcast.13, f32[1,32,128,128]{3,2,1,0:T(8,128)S(1)} %copy-done, f32[]{:T(128)} %dynamic-slice_reduce_fusion, f32[]{:T(128)} %bitcast.94), kind=kLoop, calls=%fused_computation.41 | loop fusion | flops 2097152 | bytes 6291464 | tf_op jit(solution)/shard_map/div | solution.py:61
  (1 shorter events, 0.0 us)
Async XLA Ops:
  0.0 6.5 %copy-start.5 = (bf16[1,32,128,128]{3,2,1,0:T(8,128)(2,1)S(1)}, bf16[1,32,128,128]{3,2,1,0:T(8,128)(2,1)}, u32[]{:S(2)}) copy-start(bf16[1,32,128,128]{3,2,1,0:T(8,128)(2,1)} %param.9) | copy-start | bytes 3145732
  0.0 6.5 %copy-start.4 = (bf16[1,32,128,128]{3,2,1,0:T(8,128)(2,1)S(1)}, bf16[1,32,128,128]{3,2,1,0:T(8,128)(2,1)}, u32[]{:S(2)}) copy-start(bf16[1,32,128,128]{3,2,1,0:T(8,128)(2,1)} %param.10) | copy-start | bytes 3145732
  1.0 3.7 %collective-permute-start = (bf16[2,1,1,128,128]{4,3,2,1,0:T(8,128)(2,1)S(1)}, bf16[2,1,1,128,128]{4,3,2,1,0:T(8,128)(2,1)S(1)}, u32[]{:S(2)}, u32[]{:S(2)}) collective-permute-start(bf16[2,1,1,128,128]{4,3,2,1,0:T(8,128)(2,1)S(1)} %get-tuple-element.7), channel_id=1, source_target_pairs={{0,1},{2,3},{4,5},{6,7},{8,9},{10,11},{12,13},{14,15},{16,17},{18,... | collective-permute-start | bytes 196616 | tf_op jit(solution)/shard_map/ppermute | solution.py:16
  3.3 3.1 %collective-permute-start.1 = (bf16[2,1,1,128,128]{4,3,2,1,0:T(8,128)(2,1)S(1)}, bf16[2,1,1,128,128]{4,3,2,1,0:T(8,128)(2,1)S(1)}, u32[]{:S(2)}, u32[]{:S(2)}) collective-permute-start(bf16[2,1,1,128,128]{4,3,2,1,0:T(8,128)(2,1)S(1)} %get-tuple-element.8), channel_id=1, source_target_pairs={{1,0},{3,2},{5,4},{7,6},{9,8},{11,10},{13,12},{15,14},{17,16},{19,... | collective-permute-start | bytes 196616 | tf_op jit(solution)/shard_map/ppermute | solution.py:17
  7.4 2.9 %copy-start = (f32[1,32,128,128]{3,2,1,0:T(8,128)S(1)}, f32[1,32,128,128]{3,2,1,0:T(8,128)}, u32[]{:S(2)}) copy-start(f32[1,32,128,128]{3,2,1,0:T(8,128)} %param.8) | copy-start | bytes 6291460
  7.4 2.9 %copy-start.1 = (f32[32,128,128]{2,1,0:T(8,128)S(1)}, f32[32,128,128]{2,1,0:T(8,128)}, u32[]{:S(2)}) copy-start(f32[32,128,128]{2,1,0:T(8,128)} %param.13) | copy-start | bytes 6291460
  7.5 2.9 %copy-start.2 = (f32[32,128,128]{2,1,0:T(8,128)S(1)}, f32[32,128,128]{2,1,0:T(8,128)}, u32[]{:S(2)}) copy-start(f32[32,128,128]{2,1,0:T(8,128)} %param.12) | copy-start | bytes 6291460
  7.5 3.4 %copy-start.3 = (f32[32,128,128]{2,1,0:T(8,128)S(1)}, f32[32,128,128]{2,1,0:T(8,128)}, u32[]{:S(2)}) copy-start(f32[32,128,128]{2,1,0:T(8,128)} %param.11) | copy-start | bytes 6291460
  12.1 5.2 %collective-permute-start.2 = (f32[1,1,128,128]{3,2,1,0:T(8,128)S(1)}, f32[1,1,128,128]{3,2,1,0:T(8,128)S(1)}, u32[]{:S(2)}, u32[]{:S(2)}) collective-permute-start(f32[1,1,128,128]{3,2,1,0:T(8,128)S(1)} %get-tuple-element.5), channel_id=1, source_target_pairs={{1,0},{3,2},{5,4},{7,6},{9,8},{11,10},{13,12},{15,14},{17,16},{19,... | collective-permute-start | bytes 196616 | tf_op jit(solution)/shard_map/ppermute | solution.py:17
  13.4 3.9 %collective-permute-start.3 = (f32[1,1,128,128]{3,2,1,0:T(8,128)S(1)}, f32[1,1,128,128]{3,2,1,0:T(8,128)S(1)}, u32[]{:S(2)}, u32[]{:S(2)}) collective-permute-start(f32[1,1,128,128]{3,2,1,0:T(8,128)S(1)} %get-tuple-element.6), channel_id=1, source_target_pairs={{0,1},{2,3},{4,5},{6,7},{8,9},{10,11},{12,13},{14,15},{16,17},{18,... | collective-permute-start | bytes 196616 | tf_op jit(solution)/shard_map/ppermute | solution.py:16
  67.5 3.4 %copy-start.6 = (f32[8,8]{1,0:T(8,128)S(1)}, f32[8,8]{1,0:T(8,128)}, u32[]{:S(2)}) copy-start(f32[8,8]{1,0:T(8,128)} %param.14) | copy-start | bytes 772
  77.3 52.3 %all-to-all-start.1 = ((f32[8,1,65536]{2,1,0:T(1,128)}), f32[8,1,65536]{2,1,0:T(1,128)}, u32[]{:S(2)}, u32[]{:S(2)}) async-start(f32[8,1,65536]{2,1,0:T(1,128)} %copy.11), calls=%async_computation.1 | async-start | bytes 4194304 | tf_op jit(solution)/shard_map/all_to_all | solution.py:56
where the time goes:
time: 134 us
  waiting for transfers between devices  49.1 us (37%)
  blocking collectives  32.9 us (25%)
  other arithmetic  21.9 us (16%)
  local copies, waits for them, and re-layouts  13.6 us (10%)
  starting transfers between devices  12.5 us (9%)
  matrix products  2.84 us (2%)
    all_to_all x1, waiting for transfers between devices, shards(): lax.all_to_all(mixed_cells, 'dom', split_axis=0, concat_axis=1, tiled=True)  47.2 us
    all_to_all x1, blocking collectives, shards(): lax.all_to_all(carried, 'dom', split_axis=1, concat_axis=0, tiled=True)  32.9 us
    unnamed x1, other arithmetic  8.36 us
    unnamed x17, local copies, waits for them, and re-layouts  6.47 us
    ppermute x2, starting transfers between devices, extended_2(): before = lax.ppermute(last, axis, up)  5.57 us
    all_to_all x1, starting transfers between devices, shards(): lax.all_to_all(mixed_cells, 'dom', split_axis=0, concat_axis=1, tiled=True)  4.35 us
    div x1, other arithmetic, shards(): return result / count  4.09 us
    all_to_all x1, local copies, waits for them, and re-layouts, shards(): lax.all_to_all(mixed_cells, 'dom', split_axis=0, concat_axis=1, tiled=True)  3.48 us
  transfers between devices with their start and end apart: 5, of which 2 were waited for; matrix products, arithmetic and copies ran while one was open for 1% of the time, Pallas kernels for 0%

commit v1 on v0

v1 whole, which is shorter than its diff:
```python
import functools

import jax
import jax.numpy as jnp
from jax import lax
from jax.experimental import pallas as pl
from jax.experimental.pallas import tpu as pltpu
from jax.sharding import PartitionSpec as P

misfit_weight = 8.0
f32, bf16 = jnp.float32, jnp.bfloat16
BACK = bf16
HALVES = ("a2a", "pp")
TILE = 32
VMEM = pl.BlockSpec(memory_space=pltpu.VMEM)
ANY = pl.BlockSpec(memory_space=pl.ANY)
SMEM = pl.BlockSpec(memory_space=pltpu.SMEM)
LIMIT = 48 * 1024 * 1024


def params():
    return pltpu.CompilerParams(vmem_limit_bytes=LIMIT)


def band(rows, cols, period):
    r = lax.broadcasted_iota(jnp.int32, (rows, cols), 0)
    c = lax.broadcasted_iota(jnp.int32, (rows, cols), 1)
    gap = (r % period) - (c % period)
    same = (gap == 1) | (gap == -1)
    if rows == cols and rows > period:
        same = same & (r // period == c // period)
    return jnp.where(same, 1.0, 0.0).astype(bf16)


def front_kernel(
    geometry, place, rho, p_h, s0_h, s1_h, src_h, obs_h, ab_h, halo32, halo16, *rest
):
    layers, nx, ny, start, count, parts, split = geometry
    outs, rest = rest[: parts if split else 1], rest[parts if split else 1 :]
    pv, sv, srcv, obsv, abv, w32, whl, g1, g2, nxy, axy, t2, tx, u2, ux, keep, sem = rest
    slab = place[0]
    first = max(start - 1, 0)
    final = min(start + count, layers)
    halo = final == layers
    base = first - 1
    wn = final - first + 1

    def z_of(r):
        return jnp.where(slab == 0, r, layers - 1 - r)

    def copies(r):
        k = r - base
        plain = first <= r <= final
        state0 = plain or (r == start - 1 and r >= 0)
        out = []
        if r < layers:
            z = z_of(r)
            if plain:
                for n, (src, dst) in enumerate(((p_h, pv), (src_h, srcv), (obs_h, obsv), (ab_h, abv))):
                    at = (0, z) if n == 0 else (z,)
                    out.append((src.at[at], dst.at[k], sem.at[n, k]))
            if r >= 0:
                out.append((s1_h.at[0, z], sv.at[k, :, :ny], sem.at[4, k]))
                out.append((s0_h.at[0, z], sv.at[k, :, ny:], sem.at[5, k]))
        else:
            if r == layers:
                for n, dst in enumerate((pv, srcv, obsv, abv)):
                    out.append((halo32.at[n], dst.at[k], sem.at[n, k]))
                out.append((halo16.at[2], sv.at[k, :, ny:], sem.at[5, k]))
            out.append((halo16.at[r - layers], sv.at[k, :, :ny], sem.at[4, k]))
        return [pltpu.make_async_copy(*c) for c in out]

    plan = {r: copies(r) for r in range(base, final + 2)}
    for r in plan:
        for c in plan[r]:
            c.start()
    if base < 0:
        sv[0] = jnp.zeros(sv.shape[1:], sv.dtype)
        w32[0] = jnp.zeros(w32.shape[1:], f32)
    t2[...] = band(2 * ny, 2 * ny, ny)
    u2[...] = band(2 * ny, ny, ny)
    tx[...] = band(nx, nx, nx)
    ux[...] = band(nx, 2 * nx, nx)
    own = 1.0 + rho[0]

    def forward(k):
        states = sv[k]
        nxy[...] = jnp.dot(states, t2[...], preferred_element_type=f32) + jnp.dot(
            tx[...], states, preferred_element_type=f32
        )
        for t in range(0, nx, TILE):
            rows = pl.ds(t, TILE)
            near = nxy[rows, :] + sv[k - 1, rows, :].astype(f32) + sv[k + 1, rows, :].astype(f32)
            near_one, near_zero = near[:, :ny], near[:, ny:]
            p = pv[k, rows, :]
            ab = abv[k, rows, :]
            src = srcv[k, rows, :]
            conduct = jnp.exp(p)
            inverse = 1.0 / (6.0 * conduct + ab)
            ratio = conduct * inverse
            adj_two = misfit_weight * ((src + conduct * near_one) * inverse - obsv[k, rows, :])
            weighted = ratio * adj_two
            w32[k, rows, :] = weighted
            high = weighted.astype(bf16)
            low = (weighted - high.astype(f32)).astype(bf16)
            whl[k % 2, rows, :] = high
            whl[k % 2, pl.ds(nx + t, TILE), :] = low
            scale = ratio * inverse
            six = 6.0 * src
            g1[k % 2, rows, :] = -own * p - scale * (adj_two * (ab * near_one - six))
            g2[k % 2, rows, :] = scale * (ab * near_zero - six)

    def backward(k):
        high, low = whl[k % 2, :nx, :], whl[k % 2, nx:, :]
        wide = jnp.concatenate([high, low], axis=1)
        axy[...] = jnp.dot(wide, u2[...], preferred_element_type=f32) + jnp.dot(
            ux[...], whl[k % 2], preferred_element_type=f32
        )
        for t in range(0, nx, TILE):
            rows = pl.ds(t, TILE)
            adj_one = axy[rows, :] + w32[k - 1, rows, :] + w32[k + 1, rows, :]
            out = (g1[k % 2, rows, :] - adj_one * g2[k % 2, rows, :]).astype(bf16)
            r = k + base - start
            if split:
                keep[pl.ds(pl.multiple_of(r * nx + t, TILE), TILE), :] = out
            else:
                outs[0][r, rows, :] = out

    def wait(rs):
        for r in rs:
            for c in plan[r]:
                c.wait()

    wait(range(base, first + 1))
    for r in range(first, final + 1):
        wait([r + 1])
        forward(r - base)
        if start <= r - 1 < start + count:
            backward(r - 1 - base)
    if split:
        me = place[1]
        size = count * nx // parts
        for s in range(parts):
            at = pl.multiple_of((me ^ s) * size, 16)
            outs[s][...] = keep[pl.ds(at, size), :]


def front(place, rho, arrays, halos, start, count, parts, split):
    _, layers, nx, ny = arrays[0].shape
    first = max(start - 1, 0)
    slots = min(start + count, layers) + 1 - first + 2
    geometry = (layers, nx, ny, start, count, parts, split)
    size = count * nx // parts
    if split:
        shapes = [jax.ShapeDtypeStruct((size, ny), bf16)] * parts
    else:
        shapes = [jax.ShapeDtypeStruct((count, nx, ny), bf16)]
    if halos is None:
        halos = (arrays[0], arrays[1])
    cells = (slots - 2) * nx * ny
    return pl.pallas_call(
        functools.partial(front_kernel, geometry),
        out_shape=shapes,
        in_specs=[SMEM, SMEM] + [ANY] * 8,
        out_specs=[VMEM] * len(shapes),
        scratch_shapes=[
            pltpu.VMEM((slots, nx, ny), f32),
            pltpu.VMEM((slots, nx, 2 * ny), bf16),
            pltpu.VMEM((slots, nx, ny), f32),
            pltpu.VMEM((slots, nx, ny), f32),
            pltpu.VMEM((slots, nx, ny), f32),
            pltpu.VMEM((slots, nx, ny), f32),
            pltpu.VMEM((2, 2 * nx, ny), bf16),
            pltpu.VMEM((2, nx, ny), f32),
            pltpu.VMEM((2, nx, ny), f32),
            pltpu.VMEM((nx, 2 * ny), f32),
            pltpu.VMEM((nx, ny), f32),
            pltpu.VMEM((2 * ny, 2 * ny), bf16),
            pltpu.VMEM((nx, nx), bf16),
            pltpu.VMEM((2 * ny, ny), bf16),
            pltpu.VMEM((nx, 2 * nx), bf16),
            pltpu.VMEM((count * nx if split else 16, ny), bf16),
            pltpu.SemaphoreType.DMA((6, slots)),
        ],
        compiler_params=params(),
        cost_estimate=pl.CostEstimate(flops=100 * cells, bytes_accessed=20 * cells, transcendentals=cells),
        name="front",
    )(place, rho, *arrays, *halos)


def pack_kernel(place, p_h, s0_h, s1_h, src_h, obs_h, ab_h, out32, out16, sem):
    layers = src_h.shape[0]
    face = jnp.where(place[0] == 0, layers - 1, 0)
    inner = jnp.where(place[0] == 0, layers - 2, 1)
    pairs = [
        (p_h.at[0, face], out32.at[0]),
        (src_h.at[face], out32.at[1]),
        (obs_h.at[face], out32.at[2]),
        (ab_h.at[face], out32.at[3]),
        (s1_h.at[0, face], out16.at[0]),
        (s1_h.at[0, inner], out16.at[1]),
        (s0_h.at[0, face], out16.at[2]),
    ]
    moves = [pltpu.make_async_copy(a, b, sem.at[n]) for n, (a, b) in enumerate(pairs)]
    for m in moves:
        m.start()
    for m in moves:
        m.wait()


def pack(place, arrays):
    _, layers, nx, ny = arrays[0].shape
    return pl.pallas_call(
        pack_kernel,
        out_shape=[jax.ShapeDtypeStruct((4, nx, ny), f32), jax.ShapeDtypeStruct((3, nx, ny), bf16)],
        in_specs=[SMEM] + [ANY] * 6,
        out_specs=[VMEM, VMEM],
        scratch_shapes=[pltpu.SemaphoreType.DMA((7,))],
        compiler_params=params(),
        name="pack",
    )(place, *arrays)


def mix_kernel(parts, split, place, weights, *rest):
    ins, rest = rest[: parts if split else 1], rest[parts if split else 1 :]
    outs, wide = rest[: parts if split else 1], rest[-1]
    rounded = weights[...].astype(bf16).astype(f32)
    for j in range(parts):
        for i in range(parts):
            wide[j * parts + i] = jnp.broadcast_to(rounded[j : j + 1, i : i + 1], wide.shape[1:])
    size, ny = ins[0].shape[-2:]
    me = place[1] if split else 0

    def body(step, carry):
        rows = pl.ds(pl.multiple_of(step * TILE, TILE), TILE)
        fields = []
        for s in range(parts):
            v = ins[s][rows, :] if split else ins[0][s, rows, :]
            fields.append(v.astype(f32).reshape(TILE // 8, 8, ny))
        for t in range(parts):
            total = 0.0
            for s in range(parts):
                at = (me ^ s) * parts + (me ^ t) if split else s * parts + t
                total = total + fields[s] * wide[at][None]
            out = total.reshape(TILE, ny)
            if split:
                outs[t][rows, :] = out.astype(outs[t].dtype)
            else:
                outs[0][t, rows, :] = out.astype(outs[0].dtype)
        return carry

    lax.fori_loop(0, size // TILE, body, 0)


def mix(place, weights, fields, split):
    parts = weights.shape[0]
    if split:
        shapes = [jax.ShapeDtypeStruct(f.shape, BACK if s else f32) for s, f in enumerate(fields)]
    else:
        shapes = [jax.ShapeDtypeStruct(fields[0].shape, BACK)]
    cells = parts * fields[0].shape[-2] * fields[0].shape[-1]
    return pl.pallas_call(
        functools.partial(mix_kernel, parts, split),
        out_shape=shapes,
        in_specs=[SMEM, VMEM] + [VMEM] * len(fields),
        out_specs=[VMEM] * len(shapes),
        scratch_shapes=[pltpu.VMEM((parts * parts, 8, fields[0].shape[-1]), f32)],
        compiler_params=params(),
        cost_estimate=pl.CostEstimate(flops=2 * parts * cells, bytes_accessed=4 * cells, transcendentals=0),
        name="mix",
    )(place, weights, *fields)


def last_kernel(geometry, place, rho, weights, p_h, *rest):
    layers, nx, ny, start, count, parts, split, chained = geometry
    if chained:
        rest = rest[1:]
    ins, rest = rest[: parts if split else 1], rest[parts if split else 1 :]
    out_h, pv, ov, sem_in, sem_out = rest

    def z_of(r):
        return jnp.where(place[0] == 0, r, layers - 1 - r)

    loads = [
        pltpu.make_async_copy(p_h.at[0, z_of(start + k)], pv.at[pl.ds(k * nx, nx)], sem_in.at[k])
        for k in range(count)
    ]
    stores = [
        pltpu.make_async_copy(ov.at[pl.ds(k * nx, nx)], out_h.at[0, z_of(start + k)], sem_out.at[k])
        for k in range(count)
    ]
    for c in loads:
        c.start()
    column = lax.broadcasted_iota(jnp.int32, weights.shape, 1) == place[1]
    picked = jnp.where(column, weights[...], 0.0)
    sums = jnp.sum(jnp.sum(picked, axis=1, keepdims=True), axis=0, keepdims=True)
    inverse = 1.0 / parts
    gain = rho[0] * sums * inverse

    def apply(mixed, rows):
        ov[rows, :] = mixed.astype(f32) * inverse + pv[rows, :] * gain

    if split:
        for c in loads:
            c.wait()
        size = count * nx // parts
        for s in range(parts):
            apply(ins[s][...], pl.ds(pl.multiple_of((place[1] ^ s) * size, 16), size))
        for c in stores:
            c.start()
    else:
        for k in range(count):
            loads[k].wait()
            apply(ins[0][k], pl.ds(k * nx, nx))
            stores[k].start()
    for c in stores:
        c.wait()


def last(place, rho, weights, particles, mixed, start, count, split, so_far):
    _, layers, nx, ny = particles.shape
    parts = weights.shape[0]
    chained = so_far is not None
    geometry = (layers, nx, ny, start, count, parts, split, chained)
    extra = [so_far] if chained else []
    cells = count * nx * ny
    return pl.pallas_call(
        functools.partial(last_kernel, geometry),
        out_shape=jax.ShapeDtypeStruct(particles.shape, f32),
        in_specs=[SMEM, SMEM, VMEM, ANY] + [ANY] * len(extra) + [VMEM] * len(mixed),
        out_specs=ANY,
        scratch_shapes=[
            pltpu.VMEM((count * nx, ny), f32),
            pltpu.VMEM((count * nx, ny), f32),
            pltpu.SemaphoreType.DMA((count,)),
            pltpu.SemaphoreType.DMA((count,)),
        ],
        input_output_aliases={4: 0} if chained else {},
        compiler_params=params(),
        cost_estimate=pl.CostEstimate(flops=4 * cells, bytes_accessed=10 * cells, transcendentals=0),
        name="last",
    )(place, rho, weights, particles, *extra, *mixed)


def shards(particles, state_zero, state_one, source, observed, absorb, kernel, inv_width):
    _, layers, nx, ny = particles.shape
    parts = kernel.shape[0]
    slab, me = lax.axis_index("slab"), lax.axis_index("dom")
    place = jnp.stack([slab, me]).astype(jnp.int32)
    arrays = (particles, state_zero, state_one, source, observed, absorb)

    def hop(value, s):
        return lax.ppermute(value, "dom", [(i, i ^ s) for i in range(parts)]) if s else value

    def whole(value):
        return lax.all_to_all(value, "dom", split_axis=0, concat_axis=0, tiled=True)

    order = [s for s in range(parts) if s & (parts // 2)] + [s for s in range(parts) if not s & (parts // 2)]

    def exchange(fields, split):
        if not split:
            return [whole(fields[0])]
        got = {s: hop(fields[s], s) for s in order}
        return [got[s] for s in range(parts)]

    count = layers // len(HALVES)
    faces = pack(place, arrays)
    swap = [(0, 1), (1, 0)]
    halos = [lax.ppermute(f, "slab", swap) for f in faces]
    result = None
    sent, back = [], []
    for n, kind in enumerate(HALVES):
        split = kind == "pp"
        fields = front(
            place, inv_width, arrays, halos if n == len(HALVES) - 1 else None, n * count, count, parts, split
        )
        if not split:
            fields = [fields[0].reshape(parts, -1, ny)]
        sent.append(exchange(fields, split))
    for n, kind in enumerate(HALVES):
        split = kind == "pp"
        back.append(exchange(mix(place, kernel, sent[n], split), split))
    for n, kind in enumerate(HALVES):
        split = kind == "pp"
        mixed = back[n]
        if not split:
            mixed = [mixed[0].reshape(count, nx, ny)]
        result = last(place, inv_width, kernel, particles, mixed, n * count, count, split, result)
    return result


def solution(mesh):
    return jax.shard_map(
        shards,
        mesh=mesh,
        in_specs=(
            P(("groups", "dom"), "slab", None, None),
            P(("groups", "dom"), "slab", None, None),
            P(("groups", "dom"), "slab", None, None),
            P(("groups", "slab"), None, None),
            P(("groups", "slab"), None, None),
            P(("groups", "slab"), None, None),
            P("groups", None),
            P("groups"),
        ),
        out_specs=P(("groups", "dom"), "slab", None, None),
        check_vma=False,
    )
```

time: 134 us -> 93.8 us (0.70)
  waiting for transfers between devices: 49.1 us -> 9.13 us
  Pallas kernels: 0 us -> 27.8 us
  other arithmetic: 21.9 us -> 0.08 us
  starting transfers between devices: 12.5 us -> 27.3 us
  blocking collectives: 32.9 us -> 21.9 us
  local copies, waits for them, and re-layouts: 13.6 us -> 6.06 us
  matrix products: 2.84 us -> 0 us
    all_to_all x1, waiting for transfers between devices: 47.2 us -> 0.01 us  [whole(): return lax.all_to_all(value, 'dom', split_axis=0, concat_axis=0, tiled=True)]
    pallas_call x0 -> x7, Pallas kernels: none -> 27.8 us  [the longest x2 16.4 us: front(): pl.pallas_call(functools.partial(front_kernel, geometry), out_shape=shape...]
    ppermute x4 -> x16, starting transfers between devices: 8.16 us -> 23.2 us  [the longest x14 22.6 us: hop(): lax.ppermute(value, 'dom', [(i, i ^ s) for i in range(parts)])]
    all_to_all x1, blocking collectives: 32.9 us -> 21.9 us  [whole(): return lax.all_to_all(value, 'dom', split_axis=0, concat_axis=0, tiled=True)]
    unnamed x1 -> x0, other arithmetic: 8.36 us -> none
    ppermute x4 -> x16, waiting for transfers between devices: 1.89 us -> 9.13 us  [the longest x14 7.96 us: hop(): lax.ppermute(value, 'dom', [(i, i ^ s) for i in range(parts)])]
    all_to_all x2 -> x0, local copies, waits for them, and re-layouts: 6.6 us -> none  [the longest x1 3.48 us: shards(): lax.all_to_all(mixed_cells, 'dom', split_axis=0, concat_axis=1, tiled=True)]
    div x1 -> x0, other arithmetic: 4.09 us -> none  [shards(): return result / count]
  transfers between devices with their start and end apart: 5 -> 17, of which waited for: 2 -> 4; matrix products, arithmetic and copies ran while one was open for 1% -> 0% of each run, Pallas kernels for 0% -> 16%
where the time goes in v1:
time: 93.8 us; the launch traced here: 93.1 us
  Pallas kernels  27.8 us (30%)
  starting transfers between devices  27.3 us (29%)
  blocking collectives  21.9 us (23%)
  waiting for transfers between devices  9.13 us (10%)
  local copies, waits for them, and re-layouts  6.06 us (6%)
    ppermute x14, starting transfers between devices, hop(): lax.ppermute(value, 'dom', [(i, i ^ s) for i in range(parts)])  22.6 us
    all_to_all x1, blocking collectives, whole(): return lax.all_to_all(value, 'dom', split_axis=0, concat_axis=0, tiled=True)  21.9 us
    pallas_call x2, Pallas kernels, front(): pl.pallas_call(functools.partial(front_kernel, geometry), out_shape=shape...  16.4 us
    ppermute x14, waiting for transfers between devices, hop(): lax.ppermute(value, 'dom', [(i, i ^ s) for i in range(parts)])  7.96 us
    pallas_call x2, Pallas kernels, last(): pl.pallas_call(functools.partial(last_kernel, geometry), out_shape=jax.Sh...  7.13 us
    unnamed x16, local copies, waits for them, and re-layouts  6.06 us
    all_to_all x1, starting transfers between devices, whole(): return lax.all_to_all(value, 'dom', split_axis=0, concat_axis=0, tiled=True)  4.15 us
    pallas_call x2, Pallas kernels, mix(): pl.pallas_call(functools.partial(mix_kernel, parts, split), out_shape=sha...  2.65 us
  transfers between devices with their start and end apart: 17, of which 4 were waited for; matrix products, arithmetic and copies ran while one was open for 0% of the time, Pallas kernels for 16%

profile of v1, /device:TPU:0, one launch (start us, length us, event | category | flops | bytes accessed | tf_op | source)
XLA Modules:
  0.0 93.1 jit_solution(8512678587222739416)
XLA Ops:
  0.7 0.1 pad_add_fusion.place
  0.7 0.0 copy-start
  0.7 1.6 %copy-done = f32[1,32,128,128]{3,2,1,0:T(8,128)S(1)} copy-done((f32[1,32,128,128]{3,2,1,0:T(8,128)S(1)}, f32[1,32,128,128]{3,2,1,0:T(8,128)}, u32[]{:S(2)}) %copy-start) | copy-done | bytes 2097176
  2.3 0.0 copy-start.2
  2.3 1.2 %copy-done.2 = bf16[1,32,128,128]{3,2,1,0:T(8,128)(2,1)S(1)} copy-done((bf16[1,32,128,128]{3,2,1,0:T(8,128)(2,1)S(1)}, bf16[1,32,128,128]{3,2,1,0:T(8,128)(2,1)}, u32[]{:S(2)}) %copy-start.2) | copy-done | bytes 1048600
  3.5 0.0 copy-start.4
  3.5 1.2 %copy-done.4 = bf16[1,32,128,128]{3,2,1,0:T(8,128)(2,1)S(1)} copy-done((bf16[1,32,128,128]{3,2,1,0:T(8,128)(2,1)S(1)}, bf16[1,32,128,128]{3,2,1,0:T(8,128)(2,1)}, u32[]{:S(2)}) %copy-start.4) | copy-done | bytes 1048600
  4.8 0.0 copy-start.7
  4.8 7.9 %front.2 = bf16[16,128,128]{2,1,0:T(8,128)(2,1)S(1)} custom-call(s32[2]{0:T(128)S(1)} %pad_add_fusion.place, f32[1]{0:T(128)S(6)} %copy.11.rho, f32[1,32,128,128]{3,2,1,0:T(8,128)S(1)} %copy-done, bf16[1,32,128,128]{3,2,1,0:T(8,128)(2,1)S(1)} %copy-done.2, bf16[1,32,128,128]{3,2,1,0:T(8,128)(2,1)S(1)} %copy-done.4, f32[32,128,128]{2,1,0:T(8,128)} %src_h.5, ...), custom_call_target="tpu_custom_call" | custom-call | flops 27852800 | bytes 5570560 | tf_op jit(solution)/shard_map/front/pallas_call | solution.py:161
  12.6 0.0 copy-start.1
  12.7 0.0 copy-start.3
  12.7 21.9 %all_to_all.10.rest_0_ = bf16[8,256,128]{2,1,0:T(8,128)(2,1)S(1)} all-to-all(bf16[8,256,128]{2,1,0:T(8,128)(2,1)S(1)} %bitcast.4), channel_id=1, replica_groups=mesh['groups'=2,'dom'=8,'slab'=2] {'dom'}, dimensions={0} | all-to-all | bytes 1048576 | tf_op jit(solution)/shard_map/all_to_all | solution.py:356
  34.5 0.0 copy-done.7
  34.5 1.3 %mix.2 = bf16[8,256,128]{2,1,0:T(8,128)(2,1)S(1)} custom-call(s32[2]{0:T(128)S(1)} %pad_add_fusion.place, f32[8,8]{1,0:T(8,128)S(1)} %copy-done.7, bf16[8,256,128]{2,1,0:T(8,128)(2,1)S(1)} %all_to_all.10.rest_0_), custom_call_target="tpu_custom_call" | custom-call | flops 4194304 | bytes 1048576 | tf_op jit(solution)/shard_map/mix/pallas_call | solution.py:262
  35.9 0.0 copy-start.6
  35.9 0.8 copy-done.6
  36.6 4.1 %all-to-all-start.1 = ((bf16[8,256,128]{2,1,0:T(8,128)(2,1)}), bf16[8,256,128]{2,1,0:T(8,128)(2,1)}, u32[]{:S(2)}, u32[]{:S(2)}) async-start(bf16[8,256,128]{2,1,0:T(8,128)(2,1)} %copy-done.6), calls=%async_computation.1 | async-start | bytes 1048576 | tf_op jit(solution)/shard_map/all_to_all | solution.py:356
  40.8 0.0 copy-done.1
  40.8 0.0 copy-done.3
  40.8 0.0 copy-start.5
  40.8 1.2 %copy-done.5 = bf16[1,32,128,128]{3,2,1,0:T(8,128)(2,1)S(1)} copy-done((bf16[1,32,128,128]{3,2,1,0:T(8,128)(2,1)S(1)}, bf16[1,32,128,128]{3,2,1,0:T(8,128)(2,1)}, u32[]{:S(2)}) %copy-start.5) | copy-done | bytes 1048600
  42.1 1.6 %pack.1 = (f32[4,128,128]{2,1,0:T(8,128)S(1)}, bf16[3,128,128]{2,1,0:T(8,128)(2,1)S(1)}) custom-call(s32[2]{0:T(128)S(1)} %pad_add_fusion.place, f32[1,32,128,128]{3,2,1,0:T(8,128)S(1)} %copy-done.1, bf16[1,32,128,128]{3,2,1,0:T(8,128)(2,1)S(1)} %copy-done.3, bf16[1,32,128,128]{3,2,1,0:T(8,128)(2,1)S(1)} %copy-done.5, f32[32,128,128]{2,1,0:T(8,128)} %src_h.5, ...), custom_call_target="tpu_custom_call" | custom-call | tf_op jit(solution)/shard_map/pack/pallas_call | solution.py:213
  43.7 0.1 collective-permute-start
  43.7 0.5 collective-permute-start.1
  44.2 1.2 %collective-permute-done.1.halo16 = bf16[3,128,128]{2,1,0:T(8,128)(2,1)S(1)} collective-permute-done((bf16[3,128,128]{2,1,0:T(8,128)(2,1)S(1)}, bf16[3,128,128]{2,1,0:T(8,128)(2,1)S(1)}, u32[]{:S(2)}, u32[]{:S(2)}) %collective-permute-start.1) | collective-permute-done | bytes 98336 | tf_op jit(solution)/shard_map/ppermute | solution.py:369
  45.4 0.0 collective-permute-done.halo32
  45.4 8.6 %front.3 = (bf16[256,128]{1,0:T(8,128)(2,1)S(1)}, bf16[256,128]{1,0:T(8,128)(2,1)S(1)}, bf16[256,128]{1,0:T(8,128)(2,1)S(1)}, bf16[256,128]{1,0:T(8,128)(2,1)S(1...) custom-call(s32[2]{0:T(128)S(1)} %pad_add_fusion.place, ...), custom_call_target="tpu_custom_call" | custom-call | flops 29491200 | bytes 5898240 | tf_op jit(solution)/shard_map/front/pallas_call | solution.py:161
  54.0 1.9 %collective-permute-start.2 = (bf16[256,128]{1,0:T(8,128)(2,1)S(1)}, bf16[256,128]{1,0:T(8,128)(2,1)S(1)}, u32[]{:S(2)}, u32[]{:S(2)}) collective-permute-start(bf16[256,128]{1,0:T(8,128)(2,1)S(1)} %get-tuple-element.26), channel_id=1, source_target_pairs={{0,2},{2,0},{4,6},{6,4},{8,10},{10,8},{12,14},{14,12},{1,3},{3,1},... | collective-permute-start | bytes 196616 | tf_op jit(solution)/shard_map/ppermute | solution.py:353
  55.9 1.5 %collective-permute-start.3 = (bf16[256,128]{1,0:T(8,128)(2,1)S(1)}, bf16[256,128]{1,0:T(8,128)(2,1)S(1)}, u32[]{:S(2)}, u32[]{:S(2)}) collective-permute-start(bf16[256,128]{1,0:T(8,128)(2,1)S(1)} %get-tuple-element.27), channel_id=1, source_target_pairs={{0,4},{2,6},{4,0},{6,2},{8,12},{10,14},{12,8},{14,10},{1,5},{3,7},... | collective-permute-start | bytes 196616 | tf_op jit(solution)/shard_map/ppermute | solution.py:353
  57.4 0.1 collective-permute-start.4
  57.5 2.8 %collective-permute-start.5 = (bf16[256,128]{1,0:T(8,128)(2,1)S(1)}, bf16[256,128]{1,0:T(8,128)(2,1)S(1)}, u32[]{:S(2)}, u32[]{:S(2)}) collective-permute-start(bf16[256,128]{1,0:T(8,128)(2,1)S(1)} %get-tuple-element.29), channel_id=1, source_target_pairs={{0,8},{2,10},{4,12},{6,14},{8,0},{10,2},{12,4},{14,6},{1,9},{3,11}... | collective-permute-start | bytes 196616 | tf_op jit(solution)/shard_map/ppermute | solution.py:353
  60.3 1.4 %collective-permute-start.6 = (bf16[256,128]{1,0:T(8,128)(2,1)S(1)}, bf16[256,128]{1,0:T(8,128)(2,1)S(1)}, u32[]{:S(2)}, u32[]{:S(2)}) collective-permute-start(bf16[256,128]{1,0:T(8,128)(2,1)S(1)} %get-tuple-element.30), channel_id=1, source_target_pairs={{0,10},{2,8},{4,14},{6,12},{8,2},{10,0},{12,6},{14,4},{1,11},{3,9}... | collective-permute-start | bytes 196616 | tf_op jit(solution)/shard_map/ppermute | solution.py:353
  61.8 0.0 collective-permute-done.2.rest_1_
  61.8 3.3 %collective-permute-start.7 = (bf16[256,128]{1,0:T(8,128)(2,1)S(1)}, bf16[256,128]{1,0:T(8,128)(2,1)S(1)}, u32[]{:S(2)}, u32[]{:S(2)}) collective-permute-start(bf16[256,128]{1,0:T(8,128)(2,1)S(1)} %get-tuple-element.31), channel_id=1, source_target_pairs={{0,12},{2,14},{4,8},{6,10},{8,4},{10,6},{12,0},{14,2},{1,13},{3,15... | collective-permute-start | bytes 196616 | tf_op jit(solution)/shard_map/ppermute | solution.py:353
  65.1 0.0 collective-permute-done.3.rest_2_
  65.1 0.1 collective-permute-start.8
  65.2 0.0 collective-permute-done.4.rest_3_
  65.2 0.0 collective-permute-done.5.rest_4_
  65.2 5.5 %collective-permute-done.6.rest_5_ = bf16[256,128]{1,0:T(8,128)(2,1)S(1)} collective-permute-done((bf16[256,128]{1,0:T(8,128)(2,1)S(1)}, bf16[256,128]{1,0:T(8,128)(2,1)S(1)}, u32[]{:S(2)}, u32[]{:S(2)}) %collective-permute-start.6) | collective-permute-done | bytes 65568 | tf_op jit(solution)/shard_map/ppermute | solution.py:353
  70.7 0.0 collective-permute-done.7.rest_6_
  70.7 1.5 %collective-permute-done.8.rest_7_ = bf16[256,128]{1,0:T(8,128)(2,1)S(1)} collective-permute-done((bf16[256,128]{1,0:T(8,128)(2,1)S(1)}, bf16[256,128]{1,0:T(8,128)(2,1)S(1)}, u32[]{:S(2)}, u32[]{:S(2)}) %collective-permute-start.8) | collective-permute-done | bytes 65568 | tf_op jit(solution)/shard_map/ppermute | solution.py:353
  72.1 1.3 %mix.3 = (f32[256,128]{1,0:T(8,128)S(1)}, bf16[256,128]{1,0:T(8,128)(2,1)S(1)}, bf16[256,128]{1,0:T(8,128)(2,1)S(1)}, bf16[256,128]{1,0:T(8,128)(2,1)S(1)}, bf16...) custom-call(s32[2]{0:T(128)S(1)} %pad_add_fusion.place, ...), custom_call_target="tpu_custom_call" | custom-call | flops 4194304 | bytes 1048576 | tf_op jit(solution)/shard_map/mix/pallas_call | solution.py:262
  73.5 0.6 collective-permute-start.9
  74.1 2.3 %collective-permute-start.10 = (bf16[256,128]{1,0:T(8,128)(2,1)S(1)}, bf16[256,128]{1,0:T(8,128)(2,1)S(1)}, u32[]{:S(2)}, u32[]{:S(2)}) collective-permute-start(bf16[256,128]{1,0:T(8,128)(2,1)S(1)} %get-tuple-element.35), channel_id=1, source_target_pairs={{0,4},{2,6},{4,0},{6,2},{8,12},{10,14},{12,8},{14,10},{1,5},{3,7},... | collective-permute-start | bytes 196616 | tf_op jit(solution)/shard_map/ppermute | solution.py:353
  76.4 0.6 collective-permute-start.11
  77.1 3.1 %collective-permute-start.12 = (bf16[256,128]{1,0:T(8,128)(2,1)S(1)}, bf16[256,128]{1,0:T(8,128)(2,1)S(1)}, u32[]{:S(2)}, u32[]{:S(2)}) collective-permute-start(bf16[256,128]{1,0:T(8,128)(2,1)S(1)} %get-tuple-element.37), channel_id=1, source_target_pairs={{0,8},{2,10},{4,12},{6,14},{8,0},{10,2},{12,4},{14,6},{1,9},{3,11}... | collective-permute-start | bytes 196616 | tf_op jit(solution)/shard_map/ppermute | solution.py:353
  80.2 0.1 collective-permute-start.13
  80.3 0.0 collective-permute-done.9.rest_2_
  80.3 2.3 %collective-permute-start.14 = (bf16[256,128]{1,0:T(8,128)(2,1)S(1)}, bf16[256,128]{1,0:T(8,128)(2,1)S(1)}, u32[]{:S(2)}, u32[]{:S(2)}) collective-permute-start(bf16[256,128]{1,0:T(8,128)(2,1)S(1)} %get-tuple-element.39), channel_id=1, source_target_pairs={{0,12},{2,14},{4,8},{6,10},{8,4},{10,6},{12,0},{14,2},{1,13},{3,15... | collective-permute-start | bytes 196616 | tf_op jit(solution)/shard_map/ppermute | solution.py:353
  82.5 0.0 collective-permute-done.10.rest_3_
  82.5 2.4 %collective-permute-start.15 = (bf16[256,128]{1,0:T(8,128)(2,1)S(1)}, bf16[256,128]{1,0:T(8,128)(2,1)S(1)}, u32[]{:S(2)}, u32[]{:S(2)}) collective-permute-start(bf16[256,128]{1,0:T(8,128)(2,1)S(1)} %get-tuple-element.40), channel_id=1, source_target_pairs={{0,14},{2,12},{4,10},{6,8},{8,6},{10,4},{12,2},{14,0},{1,15},{3,13... | collective-permute-start | bytes 196616 | tf_op jit(solution)/shard_map/ppermute | solution.py:353
  84.9 0.0 all-to-all-done.1
  84.9 3.7 %last.2.rest_0_ = f32[1,32,128,128]{3,2,1,0:T(8,128)} custom-call(s32[2]{0:T(128)S(1)} %pad_add_fusion.place, f32[1]{0:T(128)S(6)} %copy.11.rho, f32[8,8]{1,0:T(8,128)S(1)} %copy-done.7, f32[1,32,128,128]{3,2,1,0:T(8,128)S(1)} %copy-done.1, bf16[16,128,128]{2,1,0:T(8,128)(2,1)} %bitcast.3.rest_0_), custom_call_target="tpu_custom_call" | custom-call | flops 1048576 | bytes 2621440 | tf_op jit(solution)/shard_map/last/pallas_call | solution.py:327
  88.7 0.0 collective-permute-done.11.rest_4_
  88.7 0.0 collective-permute-done.12.rest_5_
  88.7 1.0 %collective-permute-done.13.rest_6_ = bf16[256,128]{1,0:T(8,128)(2,1)S(1)} collective-permute-done((bf16[256,128]{1,0:T(8,128)(2,1)S(1)}, bf16[256,128]{1,0:T(8,128)(2,1)S(1)}, u32[]{:S(2)}, u32[]{:S(2)}) %collective-permute-start.13) | collective-permute-done | bytes 65568 | tf_op jit(solution)/shard_map/ppermute | solution.py:353
  89.7 0.0 collective-permute-done.14.rest_7_
  89.7 0.0 collective-permute-done.15.rest_8_
  89.7 3.4 %last.3 = f32[1,32,128,128]{3,2,1,0:T(8,128)} custom-call(s32[2]{0:T(128)S(1)} %pad_add_fusion.place, f32[1]{0:T(128)S(6)} %copy.11.rho, f32[8,8]{1,0:T(8,128)S(1)} %copy-done.7, f32[1,32,128,128]{3,2,1,0:T(8,128)S(1)} %copy-done.1, f32[1,32,128,128]{3,2,1,0:T(8,128)} %last.2.rest_0_, ...), custom_call_target="tpu_custom_call", output_to_operand_aliasing={{}: (4, {})} | custom-call | flops 1048576 | bytes 2621440 | tf_op jit(solution)/shard_map/last/pallas_call | solution.py:327
Async XLA Ops:
  0.7 1.6 %copy-start = (f32[1,32,128,128]{3,2,1,0:T(8,128)S(1)}, f32[1,32,128,128]{3,2,1,0:T(8,128)}, u32[]{:S(2)}) copy-start(f32[1,32,128,128]{3,2,1,0:T(8,128)} %p_h.9) | copy-start | bytes 6291460
  2.3 1.2 %copy-start.2 = (bf16[1,32,128,128]{3,2,1,0:T(8,128)(2,1)S(1)}, bf16[1,32,128,128]{3,2,1,0:T(8,128)(2,1)}, u32[]{:S(2)}) copy-start(bf16[1,32,128,128]{3,2,1,0:T(8,128)(2,1)} %s0_h.5) | copy-start | bytes 3145732
  3.5 1.2 %copy-start.4 = (bf16[1,32,128,128]{3,2,1,0:T(8,128)(2,1)S(1)}, bf16[1,32,128,128]{3,2,1,0:T(8,128)(2,1)}, u32[]{:S(2)}) copy-start(bf16[1,32,128,128]{3,2,1,0:T(8,128)(2,1)} %s1_h.5) | copy-start | bytes 3145732
  4.8 29.8 %copy-start.7 = (f32[8,8]{1,0:T(8,128)S(1)}, f32[8,8]{1,0:T(8,128)}, u32[]{:S(2)}) copy-start(f32[8,8]{1,0:T(8,128)} %weights.7) | copy-start | bytes 772
  12.6 28.2 %copy-start.1 = (f32[1,32,128,128]{3,2,1,0:T(8,128)S(1)}, f32[1,32,128,128]{3,2,1,0:T(8,128)}, u32[]{:S(2)}) copy-start(f32[1,32,128,128]{3,2,1,0:T(8,128)} %p_h.9) | copy-start | bytes 6291460
  12.7 28.2 %copy-start.3 = (bf16[1,32,128,128]{3,2,1,0:T(8,128)(2,1)S(1)}, bf16[1,32,128,128]{3,2,1,0:T(8,128)(2,1)}, u32[]{:S(2)}) copy-start(bf16[1,32,128,128]{3,2,1,0:T(8,128)(2,1)} %s0_h.5) | copy-start | bytes 3145732
  35.9 0.8 copy-start.6
  36.6 48.3 %all-to-all-start.1 = ((bf16[8,256,128]{2,1,0:T(8,128)(2,1)}), bf16[8,256,128]{2,1,0:T(8,128)(2,1)}, u32[]{:S(2)}, u32[]{:S(2)}) async-start(bf16[8,256,128]{2,1,0:T(8,128)(2,1)} %copy-done.6), calls=%async_computation.1 | async-start | bytes 1048576 | tf_op jit(solution)/shard_map/all_to_all | solution.py:356
  40.8 1.2 %copy-start.5 = (bf16[1,32,128,128]{3,2,1,0:T(8,128)(2,1)S(1)}, bf16[1,32,128,128]{3,2,1,0:T(8,128)(2,1)}, u32[]{:S(2)}) copy-start(bf16[1,32,128,128]{3,2,1,0:T(8,128)(2,1)} %s1_h.5) | copy-start | bytes 3145732
  43.7 1.7 %collective-permute-start = (f32[4,128,128]{2,1,0:T(8,128)S(1)}, f32[4,128,128]{2,1,0:T(8,128)S(1)}, u32[]{:S(2)}, u32[]{:S(2)}) collective-permute-start(f32[4,128,128]{2,1,0:T(8,128)S(1)} %get-tuple-element.23), channel_id=1, source_target_pairs={{0,1},{1,0},{2,3},{3,2},{4,5},{5,4},{6,7},{7,6},{8,9},{9,8},{10,11... | collective-permute-start | bytes 786440 | tf_op jit(solution)/shard_map/ppermute | solution.py:369
  43.7 1.7 %collective-permute-start.1 = (bf16[3,128,128]{2,1,0:T(8,128)(2,1)S(1)}, bf16[3,128,128]{2,1,0:T(8,128)(2,1)S(1)}, u32[]{:S(2)}, u32[]{:S(2)}) collective-permute-start(bf16[3,128,128]{2,1,0:T(8,128)(2,1)S(1)} %get-tuple-element.24), channel_id=1, source_target_pairs={{0,1},{1,0},{2,3},{3,2},{4,5},{5,4},{6,7},{7,6},{8,9},{9,8},{10,11... | collective-permute-start | bytes 294920 | tf_op jit(solution)/shard_map/ppermute | solution.py:369
  54.0 7.8 %collective-permute-start.2 = (bf16[256,128]{1,0:T(8,128)(2,1)S(1)}, bf16[256,128]{1,0:T(8,128)(2,1)S(1)}, u32[]{:S(2)}, u32[]{:S(2)}) collective-permute-start(bf16[256,128]{1,0:T(8,128)(2,1)S(1)} %get-tuple-element.26), channel_id=1, source_target_pairs={{0,2},{2,0},{4,6},{6,4},{8,10},{10,8},{12,14},{14,12},{1,3},{3,1},... | collective-permute-start | bytes 196616 | tf_op jit(solution)/shard_map/ppermute | solution.py:353
  55.9 9.2 %collective-permute-start.3 = (bf16[256,128]{1,0:T(8,128)(2,1)S(1)}, bf16[256,128]{1,0:T(8,128)(2,1)S(1)}, u32[]{:S(2)}, u32[]{:S(2)}) collective-permute-start(bf16[256,128]{1,0:T(8,128)(2,1)S(1)} %get-tuple-element.27), channel_id=1, source_target_pairs={{0,4},{2,6},{4,0},{6,2},{8,12},{10,14},{12,8},{14,10},{1,5},{3,7},... | collective-permute-start | bytes 196616 | tf_op jit(solution)/shard_map/ppermute | solution.py:353
  57.4 7.8 %collective-permute-start.4 = (bf16[256,128]{1,0:T(8,128)(2,1)S(1)}, bf16[256,128]{1,0:T(8,128)(2,1)S(1)}, u32[]{:S(2)}, u32[]{:S(2)}) collective-permute-start(bf16[256,128]{1,0:T(8,128)(2,1)S(1)} %get-tuple-element.28), channel_id=1, source_target_pairs={{0,6},{2,4},{4,2},{6,0},{8,14},{10,12},{12,10},{14,8},{1,7},{3,5},... | collective-permute-start | bytes 196616 | tf_op jit(solution)/shard_map/ppermute | solution.py:353
  57.5 7.7 %collective-permute-start.5 = (bf16[256,128]{1,0:T(8,128)(2,1)S(1)}, bf16[256,128]{1,0:T(8,128)(2,1)S(1)}, u32[]{:S(2)}, u32[]{:S(2)}) collective-permute-start(bf16[256,128]{1,0:T(8,128)(2,1)S(1)} %get-tuple-element.29), channel_id=1, source_target_pairs={{0,8},{2,10},{4,12},{6,14},{8,0},{10,2},{12,4},{14,6},{1,9},{3,11}... | collective-permute-start | bytes 196616 | tf_op jit(solution)/shard_map/ppermute | solution.py:353
  60.3 10.3 %collective-permute-start.6 = (bf16[256,128]{1,0:T(8,128)(2,1)S(1)}, bf16[256,128]{1,0:T(8,128)(2,1)S(1)}, u32[]{:S(2)}, u32[]{:S(2)}) collective-permute-start(bf16[256,128]{1,0:T(8,128)(2,1)S(1)} %get-tuple-element.30), channel_id=1, source_target_pairs={{0,10},{2,8},{4,14},{6,12},{8,2},{10,0},{12,6},{14,4},{1,11},{3,9}... | collective-permute-start | bytes 196616 | tf_op jit(solution)/shard_map/ppermute | solution.py:353
  61.8 8.9 %collective-permute-start.7 = (bf16[256,128]{1,0:T(8,128)(2,1)S(1)}, bf16[256,128]{1,0:T(8,128)(2,1)S(1)}, u32[]{:S(2)}, u32[]{:S(2)}) collective-permute-start(bf16[256,128]{1,0:T(8,128)(2,1)S(1)} %get-tuple-element.31), channel_id=1, source_target_pairs={{0,12},{2,14},{4,8},{6,10},{8,4},{10,6},{12,0},{14,2},{1,13},{3,15... | collective-permute-start | bytes 196616 | tf_op jit(solution)/shard_map/ppermute | solution.py:353
  65.1 7.1 %collective-permute-start.8 = (bf16[256,128]{1,0:T(8,128)(2,1)S(1)}, bf16[256,128]{1,0:T(8,128)(2,1)S(1)}, u32[]{:S(2)}, u32[]{:S(2)}) collective-permute-start(bf16[256,128]{1,0:T(8,128)(2,1)S(1)} %get-tuple-element.32), channel_id=1, source_target_pairs={{0,14},{2,12},{4,10},{6,8},{8,6},{10,4},{12,2},{14,0},{1,15},{3,13... | collective-permute-start | bytes 196616 | tf_op jit(solution)/shard_map/ppermute | solution.py:353
  73.5 6.8 %collective-permute-start.9 = (bf16[256,128]{1,0:T(8,128)(2,1)S(1)}, bf16[256,128]{1,0:T(8,128)(2,1)S(1)}, u32[]{:S(2)}, u32[]{:S(2)}) collective-permute-start(bf16[256,128]{1,0:T(8,128)(2,1)S(1)} %get-tuple-element.34), channel_id=1, source_target_pairs={{0,2},{2,0},{4,6},{6,4},{8,10},{10,8},{12,14},{14,12},{1,3},{3,1},... | collective-permute-start | bytes 196616 | tf_op jit(solution)/shard_map/ppermute | solution.py:353
  74.1 8.4 %collective-permute-start.10 = (bf16[256,128]{1,0:T(8,128)(2,1)S(1)}, bf16[256,128]{1,0:T(8,128)(2,1)S(1)}, u32[]{:S(2)}, u32[]{:S(2)}) collective-permute-start(bf16[256,128]{1,0:T(8,128)(2,1)S(1)} %get-tuple-element.35), channel_id=1, source_target_pairs={{0,4},{2,6},{4,0},{6,2},{8,12},{10,14},{12,8},{14,10},{1,5},{3,7},... | collective-permute-start | bytes 196616 | tf_op jit(solution)/shard_map/ppermute | solution.py:353
  76.4 12.2 %collective-permute-start.11 = (bf16[256,128]{1,0:T(8,128)(2,1)S(1)}, bf16[256,128]{1,0:T(8,128)(2,1)S(1)}, u32[]{:S(2)}, u32[]{:S(2)}) collective-permute-start(bf16[256,128]{1,0:T(8,128)(2,1)S(1)} %get-tuple-element.36), channel_id=1, source_target_pairs={{0,6},{2,4},{4,2},{6,0},{8,14},{10,12},{12,10},{14,8},{1,7},{3,5},... | collective-permute-start | bytes 196616 | tf_op jit(solution)/shard_map/ppermute | solution.py:353
  77.1 11.6 %collective-permute-start.12 = (bf16[256,128]{1,0:T(8,128)(2,1)S(1)}, bf16[256,128]{1,0:T(8,128)(2,1)S(1)}, u32[]{:S(2)}, u32[]{:S(2)}) collective-permute-start(bf16[256,128]{1,0:T(8,128)(2,1)S(1)} %get-tuple-element.37), channel_id=1, source_target_pairs={{0,8},{2,10},{4,12},{6,14},{8,0},{10,2},{12,4},{14,6},{1,9},{3,11}... | collective-permute-start | bytes 196616 | tf_op jit(solution)/shard_map/ppermute | solution.py:353
  80.2 9.5 %collective-permute-start.13 = (bf16[256,128]{1,0:T(8,128)(2,1)S(1)}, bf16[256,128]{1,0:T(8,128)(2,1)S(1)}, u32[]{:S(2)}, u32[]{:S(2)}) collective-permute-start(bf16[256,128]{1,0:T(8,128)(2,1)S(1)} %get-tuple-element.38), channel_id=1, source_target_pairs={{0,10},{2,8},{4,14},{6,12},{8,2},{10,0},{12,6},{14,4},{1,11},{3,9}... | collective-permute-start | bytes 196616 | tf_op jit(solution)/shard_map/ppermute | solution.py:353
  80.3 9.4 %collective-permute-start.14 = (bf16[256,128]{1,0:T(8,128)(2,1)S(1)}, bf16[256,128]{1,0:T(8,128)(2,1)S(1)}, u32[]{:S(2)}, u32[]{:S(2)}) collective-permute-start(bf16[256,128]{1,0:T(8,128)(2,1)S(1)} %get-tuple-element.39), channel_id=1, source_target_pairs={{0,12},{2,14},{4,8},{6,10},{8,4},{10,6},{12,0},{14,2},{1,13},{3,15... | collective-permute-start | bytes 196616 | tf_op jit(solution)/shard_map/ppermute | solution.py:353
  82.5 7.1 %collective-permute-start.15 = (bf16[256,128]{1,0:T(8,128)(2,1)S(1)}, bf16[256,128]{1,0:T(8,128)(2,1)S(1)}, u32[]{:S(2)}, u32[]{:S(2)}) collective-permute-start(bf16[256,128]{1,0:T(8,128)(2,1)S(1)} %get-tuple-element.40), channel_id=1, source_target_pairs={{0,14},{2,12},{4,10},{6,8},{8,6},{10,4},{12,2},{14,0},{1,15},{3,13... | collective-permute-start | bytes 196616 | tf_op jit(solution)/shard_map/ppermute | solution.py:353

commit v2 on v0

v2 whole, which is shorter than its diff:
```python
import functools
import math

import jax
import jax.numpy as jnp
from jax import lax
from jax.experimental import pallas as pl
from jax.experimental.pallas import tpu as pltpu
from jax.sharding import PartitionSpec as P

misfit_weight = 8.0
f32, bf16 = jnp.float32, jnp.bfloat16
BACK = bf16
TILE = 32
FRONTS = ((4, 2), (4, 3), (2, 0))
GROUPS = (4, 7)
VMEM = pl.BlockSpec(memory_space=pltpu.VMEM)
ANY = pl.BlockSpec(memory_space=pl.ANY)
SMEM = pl.BlockSpec(memory_space=pltpu.SMEM)
LIMIT = 61184 * 1024
FRONT = 48 * 1024 * 1024
SMALL = 16 * 1024 * 1024


def band(rows, cols, period):
    r = lax.broadcasted_iota(jnp.int32, (rows, cols), 0)
    c = lax.broadcasted_iota(jnp.int32, (rows, cols), 1)
    gap = (r % period) - (c % period)
    same = (gap == 1) | (gap == -1)
    if rows == cols and rows > period:
        same = same & (r // period == c // period)
    return jnp.where(same, 1.0, 0.0).astype(bf16)


def pack_kernel(p_h, s0_h, s1_h, src_h, obs_h, ab_h, faces, states, sem):
    layers = src_h.shape[0]
    slab = lax.axis_index("slab")
    face = jnp.where(slab == 0, layers - 1, 0)
    inner = jnp.where(slab == 0, layers - 2, 1)
    pairs = [(p_h.at[0, face], faces.at[0]), (src_h.at[face], faces.at[1]), (obs_h.at[face], faces.at[2])]
    pairs += [(ab_h.at[face], faces.at[3]), (s1_h.at[0, face], states.at[0]), (s1_h.at[0, inner], states.at[1])]
    pairs += [(s0_h.at[0, face], states.at[2])]
    moves = [pltpu.make_async_copy(a, b, sem.at[n]) for n, (a, b) in enumerate(pairs)]
    for m in moves:
        m.start()
    for m in moves:
        m.wait()
    faces[pl.ds(4, 3)] = states[...].astype(f32)


def pack(arrays):
    _, layers, nx, ny = arrays[0].shape
    return pl.pallas_call(
        pack_kernel,
        out_shape=jax.ShapeDtypeStruct((7, nx, ny), f32),
        in_specs=[ANY] * 6,
        out_specs=VMEM,
        scratch_shapes=[pltpu.VMEM((3, nx, ny), bf16), pltpu.SemaphoreType.DMA((7,))],
        compiler_params=pltpu.CompilerParams(vmem_limit_bytes=LIMIT),
        name="pack",
    )(*arrays)


def front_kernel(geometry, rho, p_h, s0_h, s1_h, src_h, obs_h, ab_h, halo, *rest):
    rest = rest[1:] if geometry[-1] else rest
    layers, nx, ny, count, wide, parts, members, region, _ = geometry
    outs, rest = rest[: len(members)], rest[len(members) :]
    pv, sv, srcv, obsv, abv, w32, whl, g1, g2, nxy, axy, t2, tx, u2, ux, keep, hv, sem = rest
    slab, me = lax.axis_index("slab"), lax.axis_index("dom")
    group = me // len(members) ^ region
    start = group * count
    edge = jnp.clip(start - 2, 0, layers - wide)

    def slot(q):
        r = start - 2 + q
        m = r - edge
        inside = jnp.where(slab == 0, m, wide - 1 - m)
        beyond = wide + 2 if q < 2 and count == layers else wide + (0 if q in (1, count + 2) else 1)
        return jnp.where((r >= 0) & (r < layers), inside, beyond)

    waits, tops, at = [], [], 0
    while at < wide:
        n = min(GROUPS[min(len(waits), len(GROUPS) - 1)], wide - at)
        z = jnp.where(slab == 0, edge + at, layers - edge - at - n)
        into = pl.ds(jnp.where(slab == 0, at, wide - at - n), n)
        pairs = (
            (s1_h.at[0, pl.ds(z, n)], sv.at[into, :, pl.ds(0, ny)]),
            (s0_h.at[0, pl.ds(z, n)], sv.at[into, :, pl.ds(ny, ny)]),
            (p_h.at[0, pl.ds(z, n)], pv.at[into]),
            (src_h.at[pl.ds(z, n)], srcv.at[into]),
            (ab_h.at[pl.ds(z, n)], abv.at[into]),
            (obs_h.at[pl.ds(z, n)], obsv.at[into]),
        )
        waits.append([pltpu.make_async_copy(x, y, sem.at[m, len(waits)]) for m, (x, y) in enumerate(pairs)])
        at += n
        tops.append(at)
    beyond = pltpu.make_async_copy(halo, hv, sem.at[0, len(waits)])
    beyond.start()
    for copies in waits:
        for c in copies:
            c.start()
    t2[...] = band(2 * ny, 2 * ny, ny)
    u2[...] = band(2 * ny, ny, ny)
    tx[...] = band(nx, nx, nx)
    ux[...] = band(nx, 2 * nx, nx)
    own = 1.0 + rho[0]
    beyond.wait()
    face = group == layers // count - 1

    def fill(n):
        return jnp.where(face, hv[n], 0.0)

    pv[wide], srcv[wide], obsv[wide], abv[wide] = fill(0), fill(1), fill(2), jnp.where(face, hv[3], 1.0)
    sv[wide, :, :ny] = fill(4).astype(bf16)
    sv[wide + 1, :, :ny] = fill(5).astype(bf16)
    sv[wide, :, ny:] = fill(6).astype(bf16)
    sv[wide + 1, :, ny:] = jnp.zeros((nx, ny), bf16)
    sv[wide + 2] = jnp.zeros((nx, 2 * ny), bf16)
    if count == layers:
        w32[1] = jnp.zeros((nx, ny), f32)

    def near_dots(q):
        states = sv[slot(q)]
        nxy[q % 2] = jnp.dot(states, t2[...], preferred_element_type=f32) + jnp.dot(
            tx[...], states, preferred_element_type=f32
        )

    def forward(q):
        here, under, over = slot(q), slot(q - 1), slot(q + 1)
        b = q % 2
        for t in range(0, nx, TILE):
            rows = pl.ds(t, TILE)
            near = nxy[b, rows, :] + sv[under, rows, :].astype(f32) + sv[over, rows, :].astype(f32)
            near_one, near_zero = near[:, :ny], near[:, ny:]
            p = pv[here, rows, :]
            ab = abv[here, rows, :]
            src = srcv[here, rows, :]
            conduct = jnp.exp(p)
            inverse = 1.0 / (6.0 * conduct + ab)
            ratio = conduct * inverse
            adj_two = misfit_weight * ((src + conduct * near_one) * inverse - obsv[here, rows, :])
            weighted = ratio * adj_two
            if q == 1:
                weighted = jnp.where(group == 0, 0.0, weighted)
            w32[q, rows, :] = weighted
            if not 2 <= q < count + 2:
                continue
            top = weighted.astype(bf16)
            whl[b, rows, :] = top
            whl[b, pl.ds(nx + t, TILE), :] = (weighted - top.astype(f32)).astype(bf16)
            scale = ratio * inverse
            six = 6.0 * src
            g1[b, rows, :] = -own * p - scale * (adj_two * (ab * near_one - six))
            g2[b, rows, :] = scale * (ab * near_zero - six)

    def adjoint_dots(q):
        b = q % 2
        both = jnp.concatenate([whl[b, :nx, :], whl[b, nx:, :]], axis=1)
        axy[b] = jnp.dot(both, u2[...], preferred_element_type=f32) + jnp.dot(
            ux[...], whl[b], preferred_element_type=f32
        )

    def backward(q):
        b = q % 2
        for t in range(0, nx, TILE):
            rows = pl.ds(t, TILE)
            adj_one = axy[b, rows, :] + w32[q - 1, rows, :] + w32[q + 1, rows, :]
            out = (g1[b, rows, :] - adj_one * g2[b, rows, :]).astype(bf16)
            keep[pl.ds((q - 2) * nx + t, TILE), :] = out

    arrived = 0
    for q in range(1, count + 3):
        while arrived < len(waits) and (arrived == 0 or tops[arrived - 1] < min(q + 4, wide)):
            for c in waits[arrived]:
                c.wait()
            arrived += 1
        if q == 1 and count < layers:
            near_dots(q)
        if q + 1 <= count + 2:
            near_dots(q + 1)
        if q > 1 or count < layers:
            forward(q)
        if 2 <= q < count + 2:
            adjoint_dots(q)
        if q >= 3:
            backward(q - 1)
    size = layers * nx // parts
    for n, s in enumerate(members):
        at = pl.multiple_of(((me ^ s) % len(members)) * size, 16)
        outs[n][...] = keep[pl.ds(at, size), :]


def front(rho, arrays, halo, parts, pieces, region, before):
    _, layers, nx, ny = arrays[0].shape
    count = layers // pieces
    wide = min(count + 4, layers)
    width = parts // pieces
    members = tuple(range(region * width, (region + 1) * width))
    extra = [] if before is None else [before]
    geometry = (layers, nx, ny, count, wide, parts, members, region, len(extra))
    size = layers * nx // parts
    slots = wide + 3
    cells = (count + 2) * nx * ny
    return pl.pallas_call(
        functools.partial(front_kernel, geometry),
        out_shape=[jax.ShapeDtypeStruct((size, ny), bf16)] * width,
        in_specs=[SMEM] + [ANY] * (7 + len(extra)),
        out_specs=[VMEM] * width,
        scratch_shapes=[
            pltpu.VMEM((slots, nx, ny), f32),
            pltpu.VMEM((slots, nx, 2 * ny), bf16),
            pltpu.VMEM((slots, nx, ny), f32),
            pltpu.VMEM((slots, nx, ny), f32),
            pltpu.VMEM((slots, nx, ny), f32),
            pltpu.VMEM((count + 4, nx, ny), f32),
            pltpu.VMEM((2, 2 * nx, ny), bf16),
            pltpu.VMEM((2, nx, ny), f32),
            pltpu.VMEM((2, nx, ny), f32),
            pltpu.VMEM((2, nx, 2 * ny), f32),
            pltpu.VMEM((2, nx, ny), f32),
            pltpu.VMEM((2 * ny, 2 * ny), bf16),
            pltpu.VMEM((nx, nx), bf16),
            pltpu.VMEM((2 * ny, ny), bf16),
            pltpu.VMEM((nx, 2 * nx), bf16),
            pltpu.VMEM((count * nx, ny), bf16),
            pltpu.VMEM((7, nx, ny), f32),
            pltpu.SemaphoreType.DMA((6, wide // min(GROUPS) + 2)),
        ],
        compiler_params=pltpu.CompilerParams(vmem_limit_bytes=FRONT),
        cost_estimate=pl.CostEstimate(flops=100 * cells, bytes_accessed=20 * cells, transcendentals=cells),
        name="front",
    )(rho, *arrays, halo, *extra)


def mix_kernel(parts, steps, weights, *rest):
    ins, outs, wide = rest[: len(steps) or 1], rest[len(steps) or 1 : -1], rest[-1]
    rounded = weights[...].astype(bf16).astype(f32)
    for j in range(parts):
        for i in range(parts):
            wide[j * parts + i] = jnp.broadcast_to(rounded[j : j + 1, i : i + 1], wide.shape[1:])
    size, ny = ins[0].shape[-2:]
    me = lax.axis_index("dom") if steps else 0

    def body(step, carry):
        rows = pl.ds(pl.multiple_of(step * TILE, TILE), TILE)
        fields = []
        for n in range(parts):
            v = ins[n][rows, :] if steps else ins[0][n, rows, :]
            fields.append(v.astype(f32).reshape(TILE // 8, 8, ny))
        for m in range(parts):
            total = 0.0
            for n in range(parts):
                at = (me ^ steps[n]) * parts + (me ^ steps[m]) if steps else n * parts + m
                total = total + fields[n] * wide[at][None]
            out = total.reshape(TILE, ny)
            if steps:
                outs[m][rows, :] = out.astype(outs[m].dtype)
            else:
                outs[0][m, rows, :] = out.astype(outs[0].dtype)
        return carry

    lax.fori_loop(0, size // TILE, body, 0)


def mix(weights, fields, steps):
    parts = weights.shape[0]
    if steps:
        shapes = [jax.ShapeDtypeStruct(f.shape, BACK if s else f32) for s, f in zip(steps, fields)]
    else:
        shapes = [jax.ShapeDtypeStruct(fields[0].shape, BACK)]
    cells = parts * fields[0].shape[-2] * fields[0].shape[-1]
    return pl.pallas_call(
        functools.partial(mix_kernel, parts, steps),
        out_shape=shapes,
        in_specs=[VMEM] * (1 + len(fields)),
        out_specs=[VMEM] * len(shapes),
        scratch_shapes=[pltpu.VMEM((parts * parts, 8, fields[0].shape[-1]), f32)],
        compiler_params=pltpu.CompilerParams(vmem_limit_bytes=SMALL),
        cost_estimate=pl.CostEstimate(flops=2 * parts * cells, bytes_accessed=4 * cells, transcendentals=0),
        name="mix",
    )(weights, *fields)


def last_kernel(geometry, rho, weights, p, *rest):
    layers, nx, ny, start, count, parts, steps, chained = geometry
    ins, (out_h, ov, sem) = rest[: len(steps) or 1], rest[-3:]
    slab, me = lax.axis_index("slab"), lax.axis_index("dom")
    size = count * nx // parts
    column = lax.broadcasted_iota(jnp.int32, weights.shape, 1) == me
    picked = jnp.where(column, weights[...], 0.0)
    sums = jnp.sum(jnp.sum(picked, axis=1, keepdims=True), axis=0, keepdims=True)
    inverse = 1.0 / parts
    gain = rho[0] * sums * inverse
    stores = []
    pieces = [(n, (me ^ s) * size) for n, s in enumerate(steps)] or [(0, 0)]
    span = math.gcd(nx, size) if steps else nx
    for n, at in pieces:
        for t in range(0, size if steps else count * nx, span):
            row = at + t
            layer = start + row // nx
            z = jnp.where(slab == 0, layer, layers - 1 - layer)
            inside = pl.ds(pl.multiple_of(row % nx, 16), span)
            here = ins[n][pl.ds(t, span), :] if steps else ins[n][t // nx]
            place = pl.ds(len(stores) * span, span)
            ov[place, :] = here.astype(f32) * inverse + p[0, z, inside, :] * gain
            move = pltpu.make_async_copy(ov.at[place], out_h.at[0, z, inside], sem.at[len(stores)])
            move.start()
            stores.append(move)
    for c in stores:
        c.wait()


def last(rho, weights, particles, mixed, start, count, steps, so_far):
    _, layers, nx, ny = particles.shape
    parts = weights.shape[0]
    chained = so_far is not None
    geometry = (layers, nx, ny, start, count, parts, steps, chained)
    extra = [so_far] if chained else []
    size = count * nx // parts
    rows = size * len(steps) if steps else count * nx
    moves = rows // (math.gcd(nx, size) if steps else nx)
    cells = rows * ny
    return pl.pallas_call(
        functools.partial(last_kernel, geometry),
        out_shape=jax.ShapeDtypeStruct(particles.shape, f32),
        in_specs=[SMEM, VMEM, VMEM] + [VMEM] * len(mixed) + [ANY] * len(extra),
        out_specs=ANY,
        scratch_shapes=[pltpu.VMEM((rows, ny), f32), pltpu.SemaphoreType.DMA((moves,))],
        input_output_aliases={3 + len(mixed): 0} if chained else {},
        compiler_params=pltpu.CompilerParams(vmem_limit_bytes=SMALL),
        cost_estimate=pl.CostEstimate(flops=4 * cells, bytes_accessed=10 * cells, transcendentals=0),
        name="last",
    )(rho, weights, particles, *mixed, *extra)


def shards(particles, state_zero, state_one, source, observed, absorb, kernel, inv_width):
    _, layers, nx, ny = particles.shape
    parts = kernel.shape[0]
    arrays = (particles, state_zero, state_one, source, observed, absorb)
    far, near = tuple(range(parts // 2, parts)), tuple(range(1, parts // 2))
    order = (far[0], *near[:1], *far[1:], *near[1:], 0)

    def hop(value, s):
        return lax.ppermute(value, "dom", [(i, i ^ s) for i in range(parts)])

    def hops(fields):
        return [hop(fields[s], s) if s else fields[0] for s in order]

    halo = lax.ppermute(pack(arrays), "slab", [(0, 1), (1, 0)])
    fields, got = {}, [None]
    for pieces, region in FRONTS:
        width = parts // pieces
        got = front(inv_width, arrays, halo, parts, pieces, region, got[0])
        fields.update(zip(range(region * width, (region + 1) * width), got))
    got = hops(fields)
    got = dict(zip(order, mix(kernel, got, order)))
    got = dict(zip(order, hops(got)))
    return last(inv_width, kernel, particles, [got[s] for s in order], 0, layers, order, None)


def solution(mesh):
    return jax.shard_map(
        shards,
        mesh=mesh,
        in_specs=(
            P(("groups", "dom"), "slab", None, None),
            P(("groups", "dom"), "slab", None, None),
            P(("groups", "dom"), "slab", None, None),
            P(("groups", "slab"), None, None),
            P(("groups", "slab"), None, None),
            P(("groups", "slab"), None, None),
            P("groups", None),
            P("groups"),
        ),
        out_specs=P(("groups", "dom"), "slab", None, None),
        check_vma=False,
    )
```

time: 134 us -> 67.3 us (0.50)
  blocking collectives: 32.9 us -> 0 us
  waiting for transfers between devices: 49.1 us -> 23.4 us
  other arithmetic: 21.9 us -> 0 us
  Pallas kernels: 0 us -> 18.2 us
  local copies, waits for them, and re-layouts: 13.6 us -> 0.02 us
  starting transfers between devices: 12.5 us -> 24.7 us
  matrix products: 2.84 us -> 0 us
    all_to_all x1 -> x0, waiting for transfers between devices: 47.2 us -> none  [shards(): lax.all_to_all(mixed_cells, 'dom', split_axis=0, concat_axis=1, tiled=True)]
    all_to_all x1 -> x0, blocking collectives: 32.9 us -> none  [shards(): lax.all_to_all(carried, 'dom', split_axis=1, concat_axis=0, tiled=True)]
    ppermute x4 -> x15, waiting for transfers between devices: 1.89 us -> 23.4 us  [the longest x14 22.4 us: hop(): return lax.ppermute(value, 'dom', [(i, i ^ s) for i in range(parts)])]
    pallas_call x0 -> x6, Pallas kernels: none -> 18.2 us  [the longest x3 13.2 us: front(): pl.pallas_call(functools.partial(front_kernel, geometry), out_shape=[jax....]
    ppermute x4 -> x15, starting transfers between devices: 8.16 us -> 24.7 us  [the longest x14 24.2 us: hop(): return lax.ppermute(value, 'dom', [(i, i ^ s) for i in range(parts)])]
    unnamed x1 -> x0, other arithmetic: 8.36 us -> none
    all_to_all x2 -> x0, local copies, waits for them, and re-layouts: 6.6 us -> none  [the longest x1 3.48 us: shards(): lax.all_to_all(mixed_cells, 'dom', split_axis=0, concat_axis=1, tiled=True)]
    unnamed x17 -> x8, local copies, waits for them, and re-layouts: 6.47 us -> 0.02 us
  transfers between devices with their start and end apart: 5 -> 15, of which waited for: 2 -> 8; matrix products, arithmetic and copies ran while one was open for 1% -> 0% of each run, Pallas kernels for 0% -> 14%
where the time goes in v2:
time: 67.3 us; the launch traced here: 67.1 us
  starting transfers between devices  24.7 us (37%)
  waiting for transfers between devices  23.4 us (35%)
  Pallas kernels  18.2 us (27%)
  between operations  0.72 us (1%)
    ppermute x14, starting transfers between devices, hop(): return lax.ppermute(value, 'dom', [(i, i ^ s) for i in range(parts)])  24.2 us
    ppermute x14, waiting for transfers between devices, hop(): return lax.ppermute(value, 'dom', [(i, i ^ s) for i in range(parts)])  22.4 us
    pallas_call x3, Pallas kernels, front(): pl.pallas_call(functools.partial(front_kernel, geometry), out_shape=[jax....  13.2 us
    pallas_call x1, Pallas kernels, pack(): pl.pallas_call(pack_kernel, out_shape=jax.ShapeDtypeStruct((7, nx, ny), f...  1.93 us
    pallas_call x1, Pallas kernels, last(): pl.pallas_call(functools.partial(last_kernel, geometry), out_shape=jax.Sh...  1.67 us
    pallas_call x1, Pallas kernels, mix(): pl.pallas_call(functools.partial(mix_kernel, parts, steps), out_shape=sha...  1.45 us
  transfers between devices with their start and end apart: 15, of which 8 were waited for; matrix products, arithmetic and copies ran while one was open for 0% of the time, Pallas kernels for 14%

profile of v2, /device:TPU:0, one launch (start us, length us, event | category | flops | bytes accessed | tf_op | source)
XLA Modules:
  0.0 67.1 jit_solution(6485913504153297435)
XLA Ops:
  0.0 0.0 copy-start
  0.0 0.0 copy-start.2
  0.0 0.0 copy-start.1
  0.0 1.9 %pack.1 = f32[7,128,128]{2,1,0:T(8,128)} custom-call(f32[1,32,128,128]{3,2,1,0:T(8,128)} %p.1, bf16[1,32,128,128]{3,2,1,0:T(8,128)(2,1)} %s0_h.7, bf16[1,32,128,128]{3,2,1,0:T(8,128)(2,1)} %s1_h.7, f32[32,128,128]{2,1,0:T(8,128)} %src_h.7, f32[32,128,128]{2,1,0:T(8,128)} %obs_h.7, f32[32,128,128]{2,1,0:T(8,128)} %ab_h.7), custom_call_target="tpu_custom_call" | custom-call | tf_op jit(solution)/shard_map/pack/pallas_call | solution.py:53
  1.9 0.5 collective-permute-start
  3.1 1.0 %collective-permute-done.halo = f32[7,128,128]{2,1,0:T(8,128)S(1)} collective-permute-done((f32[7,128,128]{2,1,0:T(8,128)}, f32[7,128,128]{2,1,0:T(8,128)S(1)}, u32[]{:S(2)}, u32[]{:S(2)}) %collective-permute-start) | collective-permute-done | bytes 458784 | tf_op jit(solution)/shard_map/ppermute | solution.py:349
  4.1 0.0 copy-done
  4.1 0.0 copy-done.2
  4.1 0.0 copy-done.1
  4.1 3.9 %front.3 = (bf16[512,128]{1,0:T(8,128)(2,1)S(1)}, bf16[512,128]{1,0:T(8,128)(2,1)S(1)}) custom-call(f32[1]{0:T(128)S(6)} %copy.9.rho, f32[1,32,128,128]{3,2,1,0:T(8,128)S(1)} %copy-done, bf16[1,32,128,128]{3,2,1,0:T(8,128)(2,1)S(1)} %copy-done.1, bf16[1,32,128,128]{3,2,1,0:T(8,128)(2,1)S(1)} %copy-done.2, f32[32,128,128]{2,1,0:T(8,128)} %src_h.7, ...), custom_call_target="tpu_custom_call" | custom-call | flops 16384000 | bytes 3276800 | tf_op jit(solution)/shard_map/front/pallas_call | solution.py:204
  8.1 5.0 %collective-permute-start.3 = (bf16[512,128]{1,0:T(8,128)(2,1)S(1)}, bf16[512,128]{1,0:T(8,128)(2,1)S(1)}, u32[]{:S(2)}, u32[]{:S(2)}) collective-permute-start(bf16[512,128]{1,0:T(8,128)(2,1)S(1)} %get-tuple-element.24), channel_id=1, source_target_pairs={{0,10},{2,8},{4,14},{6,12},{8,2},{10,0},{12,6},{14,4},{1,11},{3,9}... | collective-permute-start | bytes 393224 | tf_op jit(solution)/shard_map/ppermute | solution.py:344
  13.1 0.3 collective-permute-start.1
  13.4 3.9 %front.4 = (bf16[512,128]{1,0:T(8,128)(2,1)S(1)}, bf16[512,128]{1,0:T(8,128)(2,1)S(1)}) custom-call(f32[1]{0:T(128)S(6)} %copy.9.rho, f32[1,32,128,128]{3,2,1,0:T(8,128)S(1)} %copy-done, bf16[1,32,128,128]{3,2,1,0:T(8,128)(2,1)S(1)} %copy-done.1, bf16[1,32,128,128]{3,2,1,0:T(8,128)(2,1)S(1)} %copy-done.2, f32[32,128,128]{2,1,0:T(8,128)} %src_h.7, ...), custom_call_target="tpu_custom_call" | custom-call | flops 16384000 | bytes 3276800 | tf_op jit(solution)/shard_map/front/pallas_call | solution.py:204
  17.4 0.0 copy-start.3
  17.4 5.3 %front.5 = (bf16[512,128]{1,0:T(8,128)(2,1)S(1)}, bf16[512,128]{1,0:T(8,128)(2,1)S(1)}, bf16[512,128]{1,0:T(8,128)(2,1)S(1)}, bf16[512,128]{1,0:T(8,128)(2,1)S(1)}) custom-call(f32[1]{0:T(128)S(6)} %copy.9.rho, f32[1,32,128,128]{3,2,1,0:T(8,128)S(1)} %copy-done, bf16[1,32,128,128]{3,2,1,0:T(8,128)(2,1)S(1)} %copy-done.1, ...), custom_call_target="tpu_custom_call" | custom-call | flops 29491200 | bytes 5898240 | tf_op jit(solution)/shard_map/front/pallas_call | solution.py:204
  22.7 0.4 collective-permute-start.2
  23.1 1.8 %collective-permute-start.6 = (bf16[512,128]{1,0:T(8,128)(2,1)S(1)}, bf16[512,128]{1,0:T(8,128)(2,1)S(1)}, u32[]{:S(2)}, u32[]{:S(2)}) collective-permute-start(bf16[512,128]{1,0:T(8,128)(2,1)S(1)} %get-tuple-element.26), channel_id=1, source_target_pairs={{0,4},{2,6},{4,0},{6,2},{8,12},{10,14},{12,8},{14,10},{1,5},{3,7},... | collective-permute-start | bytes 393224 | tf_op jit(solution)/shard_map/ppermute | solution.py:344
  24.8 1.4 %collective-permute-start.7 = (bf16[512,128]{1,0:T(8,128)(2,1)S(1)}, bf16[512,128]{1,0:T(8,128)(2,1)S(1)}, u32[]{:S(2)}, u32[]{:S(2)}) collective-permute-start(bf16[512,128]{1,0:T(8,128)(2,1)S(1)} %get-tuple-element.27), channel_id=1, source_target_pairs={{0,6},{2,4},{4,2},{6,0},{8,14},{10,12},{12,10},{14,8},{1,7},{3,5},... | collective-permute-start | bytes 393224 | tf_op jit(solution)/shard_map/ppermute | solution.py:344
  26.3 0.0 collective-permute-done.3.rest_2_
  26.3 3.5 %collective-permute-start.5 = (bf16[512,128]{1,0:T(8,128)(2,1)S(1)}, bf16[512,128]{1,0:T(8,128)(2,1)S(1)}, u32[]{:S(2)}, u32[]{:S(2)}) collective-permute-start(bf16[512,128]{1,0:T(8,128)(2,1)S(1)} %get-tuple-element.25), channel_id=1, source_target_pairs={{0,14},{2,12},{4,10},{6,8},{8,6},{10,4},{12,2},{14,0},{1,15},{3,13... | collective-permute-start | bytes 393224 | tf_op jit(solution)/shard_map/ppermute | solution.py:344
  29.8 0.0 collective-permute-done.1.rest_0_
  29.8 0.1 collective-permute-start.4
  29.9 0.0 collective-permute-done.2.rest_1_
  29.9 0.0 collective-permute-done.6.rest_5_
  29.9 1.8 %collective-permute-done.7.rest_6_ = bf16[512,128]{1,0:T(8,128)(2,1)S(1)} collective-permute-done((bf16[512,128]{1,0:T(8,128)(2,1)S(1)}, bf16[512,128]{1,0:T(8,128)(2,1)S(1)}, u32[]{:S(2)}, u32[]{:S(2)}) %collective-permute-start.7) | collective-permute-done | bytes 131104 | tf_op jit(solution)/shard_map/ppermute | solution.py:344
  31.7 6.3 %collective-permute-done.5.rest_4_ = bf16[512,128]{1,0:T(8,128)(2,1)S(1)} collective-permute-done((bf16[512,128]{1,0:T(8,128)(2,1)S(1)}, bf16[512,128]{1,0:T(8,128)(2,1)S(1)}, u32[]{:S(2)}, u32[]{:S(2)}) %collective-permute-start.5) | collective-permute-done | bytes 131104 | tf_op jit(solution)/shard_map/ppermute | solution.py:344
  38.0 1.0 %collective-permute-done.4.rest_3_ = bf16[512,128]{1,0:T(8,128)(2,1)S(1)} collective-permute-done((bf16[512,128]{1,0:T(8,128)(2,1)S(1)}, bf16[512,128]{1,0:T(8,128)(2,1)S(1)}, u32[]{:S(2)}, u32[]{:S(2)}) %collective-permute-start.4) | collective-permute-done | bytes 131104 | tf_op jit(solution)/shard_map/ppermute | solution.py:344
  39.1 0.0 copy-done.3
  39.1 1.4 %mix.1 = (bf16[512,128]{1,0:T(8,128)(2,1)S(1)}, bf16[512,128]{1,0:T(8,128)(2,1)S(1)}, bf16[512,128]{1,0:T(8,128)(2,1)S(1)}, bf16[512,128]{1,0:T(8,128)(2,1)S(1)}...) custom-call(f32[8,8]{1,0:T(8,128)S(1)} %copy-done.3, ...), custom_call_target="tpu_custom_call" | custom-call | flops 8388608 | bytes 2097152 | tf_op jit(solution)/shard_map/mix/pallas_call | solution.py:272
  40.5 2.5 %collective-permute-start.8 = (bf16[512,128]{1,0:T(8,128)(2,1)S(1)}, bf16[512,128]{1,0:T(8,128)(2,1)S(1)}, u32[]{:S(2)}, u32[]{:S(2)}) collective-permute-start(bf16[512,128]{1,0:T(8,128)(2,1)S(1)} %get-tuple-element.29), channel_id=1, source_target_pairs={{0,8},{2,10},{4,12},{6,14},{8,0},{10,2},{12,4},{14,6},{1,9},{3,11}... | collective-permute-start | bytes 393224 | tf_op jit(solution)/shard_map/ppermute | solution.py:344
  43.0 1.5 %collective-permute-start.9 = (bf16[512,128]{1,0:T(8,128)(2,1)S(1)}, bf16[512,128]{1,0:T(8,128)(2,1)S(1)}, u32[]{:S(2)}, u32[]{:S(2)}) collective-permute-start(bf16[512,128]{1,0:T(8,128)(2,1)S(1)} %get-tuple-element.30), channel_id=1, source_target_pairs={{0,2},{2,0},{4,6},{6,4},{8,10},{10,8},{12,14},{14,12},{1,3},{3,1},... | collective-permute-start | bytes 393224 | tf_op jit(solution)/shard_map/ppermute | solution.py:344
  44.5 0.5 collective-permute-start.10
  45.0 1.8 %collective-permute-start.11 = (bf16[512,128]{1,0:T(8,128)(2,1)S(1)}, bf16[512,128]{1,0:T(8,128)(2,1)S(1)}, u32[]{:S(2)}, u32[]{:S(2)}) collective-permute-start(bf16[512,128]{1,0:T(8,128)(2,1)S(1)} %get-tuple-element.32), channel_id=1, source_target_pairs={{0,12},{2,14},{4,8},{6,10},{8,4},{10,6},{12,0},{14,2},{1,13},{3,15... | collective-permute-start | bytes 393224 | tf_op jit(solution)/shard_map/ppermute | solution.py:344
  46.9 2.5 %collective-permute-start.12 = (bf16[512,128]{1,0:T(8,128)(2,1)S(1)}, bf16[512,128]{1,0:T(8,128)(2,1)S(1)}, u32[]{:S(2)}, u32[]{:S(2)}) collective-permute-start(bf16[512,128]{1,0:T(8,128)(2,1)S(1)} %get-tuple-element.33), channel_id=1, source_target_pairs={{0,14},{2,12},{4,10},{6,8},{8,6},{10,4},{12,2},{14,0},{1,15},{3,13... | collective-permute-start | bytes 393224 | tf_op jit(solution)/shard_map/ppermute | solution.py:344
  49.3 8.2 %collective-permute-done.8.rest_0_ = bf16[512,128]{1,0:T(8,128)(2,1)S(1)} collective-permute-done((bf16[512,128]{1,0:T(8,128)(2,1)S(1)}, bf16[512,128]{1,0:T(8,128)(2,1)S(1)}, u32[]{:S(2)}, u32[]{:S(2)}) %collective-permute-start.8) | collective-permute-done | bytes 131104 | tf_op jit(solution)/shard_map/ppermute | solution.py:344
  57.5 0.0 collective-permute-start.13
  57.5 0.0 collective-permute-done.9.rest_1_
  57.5 2.8 %collective-permute-start.14 = (bf16[512,128]{1,0:T(8,128)(2,1)S(1)}, bf16[512,128]{1,0:T(8,128)(2,1)S(1)}, u32[]{:S(2)}, u32[]{:S(2)}) collective-permute-start(bf16[512,128]{1,0:T(8,128)(2,1)S(1)} %get-tuple-element.35), channel_id=1, source_target_pairs={{0,6},{2,4},{4,2},{6,0},{8,14},{10,12},{12,10},{14,8},{1,7},{3,5},... | collective-permute-start | bytes 393224 | tf_op jit(solution)/shard_map/ppermute | solution.py:344
  60.3 0.7 %collective-permute-done.10.rest_2_ = bf16[512,128]{1,0:T(8,128)(2,1)S(1)} collective-permute-done((bf16[512,128]{1,0:T(8,128)(2,1)S(1)}, bf16[512,128]{1,0:T(8,128)(2,1)S(1)}, u32[]{:S(2)}, u32[]{:S(2)}) %collective-permute-start.10) | collective-permute-done | bytes 131104 | tf_op jit(solution)/shard_map/ppermute | solution.py:344
  61.1 0.0 collective-permute-done.11.rest_3_
  61.1 0.0 collective-permute-done.12.rest_4_
  61.1 2.0 %collective-permute-done.13.rest_5_ = bf16[512,128]{1,0:T(8,128)(2,1)S(1)} collective-permute-done((bf16[512,128]{1,0:T(8,128)(2,1)S(1)}, bf16[512,128]{1,0:T(8,128)(2,1)S(1)}, u32[]{:S(2)}, u32[]{:S(2)}) %collective-permute-start.13) | collective-permute-done | bytes 131104 | tf_op jit(solution)/shard_map/ppermute | solution.py:344
  63.1 2.3 %collective-permute-done.14.rest_6_ = bf16[512,128]{1,0:T(8,128)(2,1)S(1)} collective-permute-done((bf16[512,128]{1,0:T(8,128)(2,1)S(1)}, bf16[512,128]{1,0:T(8,128)(2,1)S(1)}, u32[]{:S(2)}, u32[]{:S(2)}) %collective-permute-start.14) | collective-permute-done | bytes 131104 | tf_op jit(solution)/shard_map/ppermute | solution.py:344
  65.4 1.7 %last.1 = f32[1,32,128,128]{3,2,1,0:T(8,128)} custom-call(f32[1]{0:T(128)S(6)} %copy.9.rho, f32[8,8]{1,0:T(8,128)S(1)} %copy-done.3, f32[1,32,128,128]{3,2,1,0:T(8,128)S(1)} %copy-done, bf16[512,128]{1,0:T(8,128)(2,1)S(1)} %collective-permute-done.8.rest_0_, bf16[512,128]{1,0:T(8,128)(2,1)S(1)} %collective-permute-done.9.rest_1_, ...), custom_call_target="tpu_custom_call" | custom-call | flops 2097152 | bytes 5242880 | tf_op jit(solution)/shard_map/last/pallas_call | solution.py:323
Async XLA Ops:
  0.0 4.1 %copy-start = (f32[1,32,128,128]{3,2,1,0:T(8,128)S(1)}, f32[1,32,128,128]{3,2,1,0:T(8,128)}, u32[]{:S(2)}) copy-start(f32[1,32,128,128]{3,2,1,0:T(8,128)} %p.1) | copy-start | bytes 6291460
  0.0 4.1 %copy-start.2 = (bf16[1,32,128,128]{3,2,1,0:T(8,128)(2,1)S(1)}, bf16[1,32,128,128]{3,2,1,0:T(8,128)(2,1)}, u32[]{:S(2)}) copy-start(bf16[1,32,128,128]{3,2,1,0:T(8,128)(2,1)} %s1_h.7) | copy-start | bytes 3145732
  0.0 4.1 %copy-start.1 = (bf16[1,32,128,128]{3,2,1,0:T(8,128)(2,1)S(1)}, bf16[1,32,128,128]{3,2,1,0:T(8,128)(2,1)}, u32[]{:S(2)}) copy-start(bf16[1,32,128,128]{3,2,1,0:T(8,128)(2,1)} %s0_h.7) | copy-start | bytes 3145732
  1.9 2.2 %collective-permute-start = (f32[7,128,128]{2,1,0:T(8,128)}, f32[7,128,128]{2,1,0:T(8,128)S(1)}, u32[]{:S(2)}, u32[]{:S(2)}) collective-permute-start(f32[7,128,128]{2,1,0:T(8,128)} %pack.1), channel_id=1, source_target_pairs={{0,1},{1,0},{2,3},{3,2},{4,5},{5,4},{6,7},{7,6},{8,9},{9,8},{10,11... | collective-permute-start | bytes 1376264 | tf_op jit(solution)/shard_map/ppermute | solution.py:349
  8.1 18.2 %collective-permute-start.3 = (bf16[512,128]{1,0:T(8,128)(2,1)S(1)}, bf16[512,128]{1,0:T(8,128)(2,1)S(1)}, u32[]{:S(2)}, u32[]{:S(2)}) collective-permute-start(bf16[512,128]{1,0:T(8,128)(2,1)S(1)} %get-tuple-element.24), channel_id=1, source_target_pairs={{0,10},{2,8},{4,14},{6,12},{8,2},{10,0},{12,6},{14,4},{1,11},{3,9}... | collective-permute-start | bytes 393224 | tf_op jit(solution)/shard_map/ppermute | solution.py:344
  13.1 16.7 %collective-permute-start.1 = (bf16[512,128]{1,0:T(8,128)(2,1)S(1)}, bf16[512,128]{1,0:T(8,128)(2,1)S(1)}, u32[]{:S(2)}, u32[]{:S(2)}) collective-permute-start(bf16[512,128]{1,0:T(8,128)(2,1)S(1)} %get-tuple-element.21.rest_0_), channel_id=1, source_target_pairs={{0,8},{2,10},{4,12},{6,14},{8,0},{10,2},{12,4},{14,6},{1,9},{3,11}... | collective-permute-start | bytes 393224 | tf_op jit(solution)/shard_map/ppermute | solution.py:344
  17.4 21.7 %copy-start.3 = (f32[8,8]{1,0:T(8,128)S(1)}, f32[8,8]{1,0:T(8,128)}, u32[]{:S(2)}) copy-start(f32[8,8]{1,0:T(8,128)} %weights.3) | copy-start | bytes 772
  22.7 7.2 %collective-permute-start.2 = (bf16[512,128]{1,0:T(8,128)(2,1)S(1)}, bf16[512,128]{1,0:T(8,128)(2,1)S(1)}, u32[]{:S(2)}, u32[]{:S(2)}) collective-permute-start(bf16[512,128]{1,0:T(8,128)(2,1)S(1)} %get-tuple-element.23), channel_id=1, source_target_pairs={{0,2},{2,0},{4,6},{6,4},{8,10},{10,8},{12,14},{14,12},{1,3},{3,1},... | collective-permute-start | bytes 393224 | tf_op jit(solution)/shard_map/ppermute | solution.py:344
  23.1 6.9 %collective-permute-start.6 = (bf16[512,128]{1,0:T(8,128)(2,1)S(1)}, bf16[512,128]{1,0:T(8,128)(2,1)S(1)}, u32[]{:S(2)}, u32[]{:S(2)}) collective-permute-start(bf16[512,128]{1,0:T(8,128)(2,1)S(1)} %get-tuple-element.26), channel_id=1, source_target_pairs={{0,4},{2,6},{4,0},{6,2},{8,12},{10,14},{12,8},{14,10},{1,5},{3,7},... | collective-permute-start | bytes 393224 | tf_op jit(solution)/shard_map/ppermute | solution.py:344
  24.8 6.9 %collective-permute-start.7 = (bf16[512,128]{1,0:T(8,128)(2,1)S(1)}, bf16[512,128]{1,0:T(8,128)(2,1)S(1)}, u32[]{:S(2)}, u32[]{:S(2)}) collective-permute-start(bf16[512,128]{1,0:T(8,128)(2,1)S(1)} %get-tuple-element.27), channel_id=1, source_target_pairs={{0,6},{2,4},{4,2},{6,0},{8,14},{10,12},{12,10},{14,8},{1,7},{3,5},... | collective-permute-start | bytes 393224 | tf_op jit(solution)/shard_map/ppermute | solution.py:344
  26.3 11.8 %collective-permute-start.5 = (bf16[512,128]{1,0:T(8,128)(2,1)S(1)}, bf16[512,128]{1,0:T(8,128)(2,1)S(1)}, u32[]{:S(2)}, u32[]{:S(2)}) collective-permute-start(bf16[512,128]{1,0:T(8,128)(2,1)S(1)} %get-tuple-element.25), channel_id=1, source_target_pairs={{0,14},{2,12},{4,10},{6,8},{8,6},{10,4},{12,2},{14,0},{1,15},{3,13... | collective-permute-start | bytes 393224 | tf_op jit(solution)/shard_map/ppermute | solution.py:344
  29.8 9.3 %collective-permute-start.4 = (bf16[512,128]{1,0:T(8,128)(2,1)S(1)}, bf16[512,128]{1,0:T(8,128)(2,1)S(1)}, u32[]{:S(2)}, u32[]{:S(2)}) collective-permute-start(bf16[512,128]{1,0:T(8,128)(2,1)S(1)} %get-tuple-element.22.rest_0_), channel_id=1, source_target_pairs={{0,12},{2,14},{4,8},{6,10},{8,4},{10,6},{12,0},{14,2},{1,13},{3,15... | collective-permute-start | bytes 393224 | tf_op jit(solution)/shard_map/ppermute | solution.py:344
  40.5 17.0 %collective-permute-start.8 = (bf16[512,128]{1,0:T(8,128)(2,1)S(1)}, bf16[512,128]{1,0:T(8,128)(2,1)S(1)}, u32[]{:S(2)}, u32[]{:S(2)}) collective-permute-start(bf16[512,128]{1,0:T(8,128)(2,1)S(1)} %get-tuple-element.29), channel_id=1, source_target_pairs={{0,8},{2,10},{4,12},{6,14},{8,0},{10,2},{12,4},{14,6},{1,9},{3,11}... | collective-permute-start | bytes 393224 | tf_op jit(solution)/shard_map/ppermute | solution.py:344
  43.0 14.5 %collective-permute-start.9 = (bf16[512,128]{1,0:T(8,128)(2,1)S(1)}, bf16[512,128]{1,0:T(8,128)(2,1)S(1)}, u32[]{:S(2)}, u32[]{:S(2)}) collective-permute-start(bf16[512,128]{1,0:T(8,128)(2,1)S(1)} %get-tuple-element.30), channel_id=1, source_target_pairs={{0,2},{2,0},{4,6},{6,4},{8,10},{10,8},{12,14},{14,12},{1,3},{3,1},... | collective-permute-start | bytes 393224 | tf_op jit(solution)/shard_map/ppermute | solution.py:344
  44.5 16.5 %collective-permute-start.10 = (bf16[512,128]{1,0:T(8,128)(2,1)S(1)}, bf16[512,128]{1,0:T(8,128)(2,1)S(1)}, u32[]{:S(2)}, u32[]{:S(2)}) collective-permute-start(bf16[512,128]{1,0:T(8,128)(2,1)S(1)} %get-tuple-element.31), channel_id=1, source_target_pairs={{0,10},{2,8},{4,14},{6,12},{8,2},{10,0},{12,6},{14,4},{1,11},{3,9}... | collective-permute-start | bytes 393224 | tf_op jit(solution)/shard_map/ppermute | solution.py:344
  45.0 16.1 %collective-permute-start.11 = (bf16[512,128]{1,0:T(8,128)(2,1)S(1)}, bf16[512,128]{1,0:T(8,128)(2,1)S(1)}, u32[]{:S(2)}, u32[]{:S(2)}) collective-permute-start(bf16[512,128]{1,0:T(8,128)(2,1)S(1)} %get-tuple-element.32), channel_id=1, source_target_pairs={{0,12},{2,14},{4,8},{6,10},{8,4},{10,6},{12,0},{14,2},{1,13},{3,15... | collective-permute-start | bytes 393224 | tf_op jit(solution)/shard_map/ppermute | solution.py:344
  46.9 14.2 %collective-permute-start.12 = (bf16[512,128]{1,0:T(8,128)(2,1)S(1)}, bf16[512,128]{1,0:T(8,128)(2,1)S(1)}, u32[]{:S(2)}, u32[]{:S(2)}) collective-permute-start(bf16[512,128]{1,0:T(8,128)(2,1)S(1)} %get-tuple-element.33), channel_id=1, source_target_pairs={{0,14},{2,12},{4,10},{6,8},{8,6},{10,4},{12,2},{14,0},{1,15},{3,13... | collective-permute-start | bytes 393224 | tf_op jit(solution)/shard_map/ppermute | solution.py:344
  57.5 5.5 %collective-permute-start.13 = (bf16[512,128]{1,0:T(8,128)(2,1)S(1)}, bf16[512,128]{1,0:T(8,128)(2,1)S(1)}, u32[]{:S(2)}, u32[]{:S(2)}) collective-permute-start(bf16[512,128]{1,0:T(8,128)(2,1)S(1)} %get-tuple-element.34), channel_id=1, source_target_pairs={{0,4},{2,6},{4,0},{6,2},{8,12},{10,14},{12,8},{14,10},{1,5},{3,7},... | collective-permute-start | bytes 393224 | tf_op jit(solution)/shard_map/ppermute | solution.py:344
  57.5 7.8 %collective-permute-start.14 = (bf16[512,128]{1,0:T(8,128)(2,1)S(1)}, bf16[512,128]{1,0:T(8,128)(2,1)S(1)}, u32[]{:S(2)}, u32[]{:S(2)}) collective-permute-start(bf16[512,128]{1,0:T(8,128)(2,1)S(1)} %get-tuple-element.35), channel_id=1, source_target_pairs={{0,6},{2,4},{4,2},{6,0},{8,14},{10,12},{12,10},{14,8},{1,7},{3,5},... | collective-permute-start | bytes 393224 | tf_op jit(solution)/shard_map/ppermute | solution.py:344

commit v3 on v2

--- a/solution.py
+++ b/solution.py
@@ -12,8 +12,11 @@
 f32, bf16 = jnp.float32, jnp.bfloat16
 BACK = bf16
 TILE = 32
-FRONTS = ((4, 2), (4, 3), (2, 0))
-GROUPS = (4, 7)
+INORDER = lambda f, n: (*f[len(f)//2:], *f[:len(f)//2], *n)
+HELD = ()
+LOAD = 54 * 1024 * 1024
+FRONTS = ((4, 2), (2, 0), (4, 3))
+GROUPS = (6, 7)
 VMEM = pl.BlockSpec(memory_space=pltpu.VMEM)
 ANY = pl.BlockSpec(memory_space=pl.ANY)
 SMEM = pl.BlockSpec(memory_space=pltpu.SMEM)
@@ -61,97 +64,142 @@
     )(*arrays)
 
 
-def front_kernel(geometry, rho, p_h, s0_h, s1_h, src_h, obs_h, ab_h, halo, *rest):
-    rest = rest[1:] if geometry[-1] else rest
-    layers, nx, ny, count, wide, parts, members, region, _ = geometry
-    outs, rest = rest[: len(members)], rest[len(members) :]
-    pv, sv, srcv, obsv, abv, w32, whl, g1, g2, nxy, axy, t2, tx, u2, ux, keep, hv, sem = rest
+def window(layers, count, group):
+    wide = min(count + 4, layers)
+    return wide, jnp.clip(group * count - 2, 0, layers - wide)
+
+
+def load_kernel(layers, count, width, region, *refs):
+    sources, held, sem = refs[:3], refs[3:6], refs[6]
+    slab, me = lax.axis_index("slab"), lax.axis_index("dom")
+    wide, edge = window(layers, count, me // width ^ region)
+    z = pl.ds(jnp.where(slab == 0, edge, layers - edge - wide), wide)
+    moves = [pltpu.make_async_copy(x.at[z], y, sem.at[n]) for n, (x, y) in enumerate(zip(sources, held))]
+    for m in moves:
+        m.start()
+    for m in moves:
+        m.wait()
+
+
+def load(fields, parts, pieces, region):
+    layers, nx, ny = fields[0].shape
+    count = layers // pieces
+    wide = min(count + 4, layers)
+    return pl.pallas_call(
+        functools.partial(load_kernel, layers, count, parts // pieces, region),
+        out_shape=[jax.ShapeDtypeStruct((wide, nx, ny), f32)] * 3,
+        in_specs=[ANY] * 3,
+        out_specs=[VMEM] * 3,
+        scratch_shapes=[pltpu.SemaphoreType.DMA((3,))],
+        compiler_params=pltpu.CompilerParams(vmem_limit_bytes=LOAD),
+        cost_estimate=pl.CostEstimate(flops=0, bytes_accessed=24 * wide * nx * ny, transcendentals=0),
+        name="load",
+    )(*fields)
+
+
+def front_kernel(geometry, rho, p, s0, s1, src, obs, ab, halo, *rest):
+    layers, nx, ny, count, parts, members, region, held, skip = geometry
+    outs, rest = rest[skip : skip + len(members)], rest[skip + len(members) :]
+    if not held:
+        here, sem, rest = rest[:3], rest[3], rest[4:]
+    w32, whl, g1, g2, nxy, axy, t2, tx, u2, ux, keep, pe, srce, obse, abe, se = rest
     slab, me = lax.axis_index("slab"), lax.axis_index("dom")
     group = me // len(members) ^ region
     start = group * count
-    edge = jnp.clip(start - 2, 0, layers - wide)
-
-    def slot(q):
-        r = start - 2 + q
-        m = r - edge
-        inside = jnp.where(slab == 0, m, wide - 1 - m)
-        beyond = wide + 2 if q < 2 and count == layers else wide + (0 if q in (1, count + 2) else 1)
-        return jnp.where((r >= 0) & (r < layers), inside, beyond)
-
-    waits, tops, at = [], [], 0
-    while at < wide:
-        n = min(GROUPS[min(len(waits), len(GROUPS) - 1)], wide - at)
-        z = jnp.where(slab == 0, edge + at, layers - edge - at - n)
-        into = pl.ds(jnp.where(slab == 0, at, wide - at - n), n)
-        pairs = (
-            (s1_h.at[0, pl.ds(z, n)], sv.at[into, :, pl.ds(0, ny)]),
-            (s0_h.at[0, pl.ds(z, n)], sv.at[into, :, pl.ds(ny, ny)]),
-            (p_h.at[0, pl.ds(z, n)], pv.at[into]),
-            (src_h.at[pl.ds(z, n)], srcv.at[into]),
-            (ab_h.at[pl.ds(z, n)], abv.at[into]),
-            (obs_h.at[pl.ds(z, n)], obsv.at[into]),
-        )
-        waits.append([pltpu.make_async_copy(x, y, sem.at[m, len(waits)]) for m, (x, y) in enumerate(pairs)])
-        at += n
-        tops.append(at)
-    beyond = pltpu.make_async_copy(halo, hv, sem.at[0, len(waits)])
-    beyond.start()
-    for copies in waits:
-        for c in copies:
-            c.start()
     t2[...] = band(2 * ny, 2 * ny, ny)
     u2[...] = band(2 * ny, ny, ny)
     tx[...] = band(nx, nx, nx)
     ux[...] = band(nx, 2 * nx, nx)
     own = 1.0 + rho[0]
-    beyond.wait()
-    face = group == layers // count - 1
-
-    def fill(n):
-        return jnp.where(face, hv[n], 0.0)
-
-    pv[wide], srcv[wide], obsv[wide], abv[wide] = fill(0), fill(1), fill(2), jnp.where(face, hv[3], 1.0)
-    sv[wide, :, :ny] = fill(4).astype(bf16)
-    sv[wide + 1, :, :ny] = fill(5).astype(bf16)
-    sv[wide, :, ny:] = fill(6).astype(bf16)
-    sv[wide + 1, :, ny:] = jnp.zeros((nx, ny), bf16)
-    sv[wide + 2] = jnp.zeros((nx, 2 * ny), bf16)
-    if count == layers:
-        w32[1] = jnp.zeros((nx, ny), f32)
+    low, high = group == 0, group == layers // count - 1
+
+    wide, edge = window(layers, count, group)
+    waits, tops = [], []
+    if not held:
+        at = 0
+        while at < wide:
+            n = min(GROUPS[min(len(waits), len(GROUPS) - 1)], wide - at)
+            z = pl.ds(jnp.where(slab == 0, edge + at, layers - edge - at - n), n)
+            into = pl.ds(jnp.where(slab == 0, at, wide - at - n), n)
+            pairs = zip((src, obs, ab), here)
+            waits.append([pltpu.make_async_copy(x.at[z], y.at[into], sem.at[m, len(waits)]) for m, (x, y) in enumerate(pairs)])
+            at += n
+            tops.append(at)
+        for copies in waits:
+            for c in copies:
+                c.start()
+        src, obs, ab = here
+
+    def z_of(q):
+        r = jnp.clip(start - 2 + q, 0, layers - 1)
+        return jnp.where(slab == 0, r, layers - 1 - r)
+
+    def w_of(q):
+        m = jnp.clip(start - 2 + q, 0, layers - 1) - edge
+        return jnp.where(slab == 0, m, wide - 1 - m)
+
+    for e, q in enumerate((0, 1, count + 2, count + 3)):
+        z = z_of(q)
+        outer = low if e < 2 else high
+        one = jnp.where(outer, 0.0 if e < 2 else halo[4 if e == 2 else 5], s1[0, z].astype(f32))
+        zero = jnp.where(outer, 0.0 if e < 2 else halo[6], s0[0, z].astype(f32))
+        se[e, :, :ny] = one.astype(bf16)
+        se[e, :, ny:] = zero.astype(bf16)
+
+    def border(q):
+        z, w = z_of(q), w_of(q)
+        e = 0 if q == 1 else 1
+        pe[e] = jnp.where(high, halo[0], p[0, z]) if e else p[0, z]
+        srce[e] = jnp.where(high, halo[1], src[w]) if e else src[w]
+        obse[e] = jnp.where(high, halo[2], obs[w]) if e else obs[w]
+        abe[e] = jnp.where(high, halo[3], ab[w]) if e else ab[w]
+
+    def inside(q):
+        return 2 <= q < count + 2
+
+    def states(q, rows):
+        if inside(q):
+            z = z_of(q)
+            return jnp.concatenate([s1[0, z, rows, :], s0[0, z, rows, :]], axis=1)
+        return se[q if q < 2 else q - count, rows, :]
+
+    def fields(q, rows):
+        if inside(q):
+            w = w_of(q)
+            return p[0, z_of(q), rows, :], src[w, rows, :], obs[w, rows, :], ab[w, rows, :]
+        e = 0 if q == 1 else 1
+        return pe[e, rows, :], srce[e, rows, :], obse[e, rows, :], abe[e, rows, :]
 
     def near_dots(q):
-        states = sv[slot(q)]
-        nxy[q % 2] = jnp.dot(states, t2[...], preferred_element_type=f32) + jnp.dot(
-            tx[...], states, preferred_element_type=f32
+        here = states(q, slice(None))
+        nxy[q % 2] = jnp.dot(here, t2[...], preferred_element_type=f32) + jnp.dot(
+            tx[...], here, preferred_element_type=f32
         )
 
     def forward(q):
-        here, under, over = slot(q), slot(q - 1), slot(q + 1)
         b = q % 2
         for t in range(0, nx, TILE):
             rows = pl.ds(t, TILE)
-            near = nxy[b, rows, :] + sv[under, rows, :].astype(f32) + sv[over, rows, :].astype(f32)
+            near = nxy[b, rows, :] + states(q - 1, rows).astype(f32) + states(q + 1, rows).astype(f32)
             near_one, near_zero = near[:, :ny], near[:, ny:]
-            p = pv[here, rows, :]
-            ab = abv[here, rows, :]
-            src = srcv[here, rows, :]
-            conduct = jnp.exp(p)
-            inverse = 1.0 / (6.0 * conduct + ab)
+            log_field, supply, seen, decay = fields(q, rows)
+            conduct = jnp.exp(log_field)
+            inverse = 1.0 / (6.0 * conduct + decay)
             ratio = conduct * inverse
-            adj_two = misfit_weight * ((src + conduct * near_one) * inverse - obsv[here, rows, :])
+            adj_two = misfit_weight * ((supply + conduct * near_one) * inverse - seen)
             weighted = ratio * adj_two
             if q == 1:
-                weighted = jnp.where(group == 0, 0.0, weighted)
+                weighted = jnp.where(low, 0.0, weighted)
             w32[q, rows, :] = weighted
-            if not 2 <= q < count + 2:
+            if not inside(q):
                 continue
             top = weighted.astype(bf16)
             whl[b, rows, :] = top
             whl[b, pl.ds(nx + t, TILE), :] = (weighted - top.astype(f32)).astype(bf16)
             scale = ratio * inverse
-            six = 6.0 * src
-            g1[b, rows, :] = -own * p - scale * (adj_two * (ab * near_one - six))
-            g2[b, rows, :] = scale * (ab * near_zero - six)
+            six = 6.0 * supply
+            g1[b, rows, :] = -own * log_field - scale * (adj_two * (decay * near_one - six))
+            g2[b, rows, :] = scale * (decay * near_zero - six)
 
     def adjoint_dots(q):
         b = q % 2
@@ -169,18 +217,18 @@
             keep[pl.ds((q - 2) * nx + t, TILE), :] = out
 
     arrived = 0
+    near_dots(1)
     for q in range(1, count + 3):
-        while arrived < len(waits) and (arrived == 0 or tops[arrived - 1] < min(q + 4, wide)):
+        while arrived < len(waits) and (arrived == 0 or tops[arrived - 1] < min(q + 3, wide)):
             for c in waits[arrived]:
                 c.wait()
             arrived += 1
-        if q == 1 and count < layers:
-            near_dots(q)
+        if not inside(q):
+            border(q)
         if q + 1 <= count + 2:
             near_dots(q + 1)
-        if q > 1 or count < layers:
-            forward(q)
-        if 2 <= q < count + 2:
+        forward(q)
+        if inside(q):
             adjoint_dots(q)
         if q >= 3:
             backward(q - 1)
@@ -192,26 +240,24 @@
 
 def front(rho, arrays, halo, parts, pieces, region, before):
     _, layers, nx, ny = arrays[0].shape
+    deep = arrays[3].shape[0]
     count = layers // pieces
-    wide = min(count + 4, layers)
     width = parts // pieces
     members = tuple(range(region * width, (region + 1) * width))
     extra = [] if before is None else [before]
-    geometry = (layers, nx, ny, count, wide, parts, members, region, len(extra))
+    held = deep < layers
+    wide = min(count + 4, layers)
+    local = [] if held else [pltpu.VMEM((wide, nx, ny), f32)] * 3 + [pltpu.SemaphoreType.DMA((3, wide // min(GROUPS) + 1))]
+    geometry = (layers, nx, ny, count, parts, members, region, held, len(extra))
     size = layers * nx // parts
-    slots = wide + 3
     cells = (count + 2) * nx * ny
     return pl.pallas_call(
         functools.partial(front_kernel, geometry),
         out_shape=[jax.ShapeDtypeStruct((size, ny), bf16)] * width,
-        in_specs=[SMEM] + [ANY] * (7 + len(extra)),
+        in_specs=[SMEM] + [VMEM] * 3 + [VMEM if held else ANY] * 3 + [VMEM] + [ANY] * len(extra),
         out_specs=[VMEM] * width,
-        scratch_shapes=[
-            pltpu.VMEM((slots, nx, ny), f32),
-            pltpu.VMEM((slots, nx, 2 * ny), bf16),
-            pltpu.VMEM((slots, nx, ny), f32),
-            pltpu.VMEM((slots, nx, ny), f32),
-            pltpu.VMEM((slots, nx, ny), f32),
+        scratch_shapes=local
+        + [
             pltpu.VMEM((count + 4, nx, ny), f32),
             pltpu.VMEM((2, 2 * nx, ny), bf16),
             pltpu.VMEM((2, nx, ny), f32),
@@ -223,54 +269,64 @@
             pltpu.VMEM((2 * ny, ny), bf16),
             pltpu.VMEM((nx, 2 * nx), bf16),
             pltpu.VMEM((count * nx, ny), bf16),
-            pltpu.VMEM((7, nx, ny), f32),
-            pltpu.SemaphoreType.DMA((6, wide // min(GROUPS) + 2)),
+            pltpu.VMEM((2, nx, ny), f32),
+            pltpu.VMEM((2, nx, ny), f32),
+            pltpu.VMEM((2, nx, ny), f32),
+            pltpu.VMEM((2, nx, ny), f32),
+            pltpu.VMEM((4, nx, 2 * ny), bf16),
         ],
         compiler_params=pltpu.CompilerParams(vmem_limit_bytes=FRONT),
-        cost_estimate=pl.CostEstimate(flops=100 * cells, bytes_accessed=20 * cells, transcendentals=cells),
+        cost_estimate=pl.CostEstimate(flops=100 * cells, bytes_accessed=70 * cells, transcendentals=cells),
         name="front",
     )(rho, *arrays, halo, *extra)
 
 
-def mix_kernel(parts, steps, weights, *rest):
-    ins, outs, wide = rest[: len(steps) or 1], rest[len(steps) or 1 : -1], rest[-1]
+def gate_kernel(*refs):
+    refs[-1][...] = jnp.zeros_like(refs[-1])
+
+
+def gate(fields):
+    return pl.pallas_call(
+        gate_kernel,
+        out_shape=jax.ShapeDtypeStruct((8, 128), f32),
+        in_specs=[ANY] * len(fields),
+        out_specs=VMEM,
+        compiler_params=pltpu.CompilerParams(vmem_limit_bytes=SMALL),
+        cost_estimate=pl.CostEstimate(flops=1000, bytes_accessed=2000000, transcendentals=0),
+        name="gate",
+    )(*fields)
+
+
+def mix_kernel(parts, steps, members, weights, *rest):
+    ins, outs, wide = rest[:parts], rest[parts:-1], rest[-1]
     rounded = weights[...].astype(bf16).astype(f32)
     for j in range(parts):
         for i in range(parts):
             wide[j * parts + i] = jnp.broadcast_to(rounded[j : j + 1, i : i + 1], wide.shape[1:])
     size, ny = ins[0].shape[-2:]
-    me = lax.axis_index("dom") if steps else 0
+    me = lax.axis_index("dom")
 
     def body(step, carry):
         rows = pl.ds(pl.multiple_of(step * TILE, TILE), TILE)
         fields = []
         for n in range(parts):
-            v = ins[n][rows, :] if steps else ins[0][n, rows, :]
-            fields.append(v.astype(f32).reshape(TILE // 8, 8, ny))
-        for m in range(parts):
+            fields.append(ins[n][rows, :].astype(f32).reshape(TILE // 8, 8, ny))
+        for m, target in enumerate(members):
             total = 0.0
-            for n in range(parts):
-                at = (me ^ steps[n]) * parts + (me ^ steps[m]) if steps else n * parts + m
-                total = total + fields[n] * wide[at][None]
-            out = total.reshape(TILE, ny)
-            if steps:
-                outs[m][rows, :] = out.astype(outs[m].dtype)
-            else:
-                outs[0][m, rows, :] = out.astype(outs[0].dtype)
+            for n, s in enumerate(steps):
+                total = total + fields[n] * wide[(me ^ s) * parts + (me ^ target)][None]
+            outs[m][rows, :] = total.reshape(TILE, ny).astype(outs[m].dtype)
         return carry
 
     lax.fori_loop(0, size // TILE, body, 0)
 
 
-def mix(weights, fields, steps):
+def mix(weights, fields, steps, members):
     parts = weights.shape[0]
-    if steps:
-        shapes = [jax.ShapeDtypeStruct(f.shape, BACK if s else f32) for s, f in zip(steps, fields)]
-    else:
-        shapes = [jax.ShapeDtypeStruct(fields[0].shape, BACK)]
+    shapes = [jax.ShapeDtypeStruct(fields[0].shape, BACK if s else f32) for s in members]
     cells = parts * fields[0].shape[-2] * fields[0].shape[-1]
     return pl.pallas_call(
-        functools.partial(mix_kernel, parts, steps),
+        functools.partial(mix_kernel, parts, steps, members),
         out_shape=shapes,
         in_specs=[VMEM] * (1 + len(fields)),
         out_specs=[VMEM] * len(shapes),
@@ -343,18 +399,20 @@
     def hop(value, s):
         return lax.ppermute(value, "dom", [(i, i ^ s) for i in range(parts)])
 
-    def hops(fields):
+    def hops(fields, order):
         return [hop(fields[s], s) if s else fields[0] for s in order]
 
     halo = lax.ppermute(pack(arrays), "slab", [(0, 1), (1, 0)])
     fields, got = {}, [None]
-    for pieces, region in FRONTS:
+    for n, (pieces, region) in enumerate(FRONTS):
         width = parts // pieces
-        got = front(inv_width, arrays, halo, parts, pieces, region, got[0])
+        inputs = arrays[:3] + tuple(load(arrays[3:], parts, pieces, region)) if n in HELD else arrays
+        got = front(inv_width, inputs, halo, parts, pieces, region, got[0])
         fields.update(zip(range(region * width, (region + 1) * width), got))
-    got = hops(fields)
-    got = dict(zip(order, mix(kernel, got, order)))
-    got = dict(zip(order, hops(got)))
+    lead = tuple(INORDER(far, near)) + (0,)
+    got = hops(fields, lead)
+    got = dict(zip(order, mix(kernel, got, lead, order)))
+    got = dict(zip(order, hops(got, order)))
     return last(inv_width, kernel, particles, [got[s] for s in order], 0, layers, order, None)
 
 

time: 67.3 us -> 65.1 us (0.967)
  Pallas kernels: 18.2 us -> 15 us
  starting transfers between devices: 24.7 us -> 25.7 us
    pallas_call x3, Pallas kernels: 13.2 us -> 9.91 us  [front(): pl.pallas_call(functools.partial(front_kernel, geometry), out_shape=[jax....]
    ppermute x14, starting transfers between devices: 24.2 us -> 25.2 us  [hop(): return lax.ppermute(value, 'dom', [(i, i ^ s) for i in range(parts)])]
  transfers between devices with their start and end apart: 15 -> 15, of which waited for: 8 -> 7; matrix products, arithmetic and copies ran while one was open for 0% -> 0% of each run, Pallas kernels for 14% -> 11%
where the time goes in v3:
time: 65.1 us; the launch traced here: 64.9 us
  starting transfers between devices  25.7 us (39%)
  waiting for transfers between devices  23.5 us (36%)
  Pallas kernels  15 us (23%)
  between operations  0.72 us (1%)
    ppermute x14, starting transfers between devices, hop(): return lax.ppermute(value, 'dom', [(i, i ^ s) for i in range(parts)])  25.2 us
    ppermute x14, waiting for transfers between devices, hop(): return lax.ppermute(value, 'dom', [(i, i ^ s) for i in range(parts)])  22.5 us
    pallas_call x3, Pallas kernels, front(): pl.pallas_call(functools.partial(front_kernel, geometry), out_shape=[jax....  9.91 us
    pallas_call x1, Pallas kernels, pack(): pl.pallas_call(pack_kernel, out_shape=jax.ShapeDtypeStruct((7, nx, ny), f...  1.93 us
    pallas_call x1, Pallas kernels, last(): pl.pallas_call(functools.partial(last_kernel, geometry), out_shape=jax.Sh...  1.67 us
    pallas_call x1, Pallas kernels, mix(): pl.pallas_call(functools.partial(mix_kernel, parts, steps, members), out_...  1.46 us
  transfers between devices with their start and end apart: 15, of which 7 were waited for; matrix products, arithmetic and copies ran while one was open for 0% of the time, Pallas kernels for 11%

profile of v3, /device:TPU:0, one launch (start us, length us, event | category | flops | bytes accessed | tf_op | source)
XLA Modules:
  0.0 64.9 jit_solution(2128571871211368915)
XLA Ops:
  0.0 0.0 copy-start
  0.0 0.0 copy-start.2
  0.0 0.0 copy-start.1
  0.0 1.9 %pack.1 = f32[7,128,128]{2,1,0:T(8,128)} custom-call(f32[1,32,128,128]{3,2,1,0:T(8,128)} %p.7, bf16[1,32,128,128]{3,2,1,0:T(8,128)(2,1)} %s0.5, bf16[1,32,128,128]{3,2,1,0:T(8,128)(2,1)} %s1_.5, f32[32,128,128]{2,1,0:T(8,128)} %src.5, f32[32,128,128]{2,1,0:T(8,128)} %obs.5, f32[32,128,128]{2,1,0:T(8,128)} %ab.5), custom_call_target="tpu_custom_call" | custom-call | tf_op jit(solution)/shard_map/pack/pallas_call | solution.py:56
  1.9 0.5 collective-permute-start
  3.1 1.0 %collective-permute-done.halo = f32[7,128,128]{2,1,0:T(8,128)S(1)} collective-permute-done((f32[7,128,128]{2,1,0:T(8,128)}, f32[7,128,128]{2,1,0:T(8,128)S(1)}, u32[]{:S(2)}, u32[]{:S(2)}) %collective-permute-start) | collective-permute-done | bytes 458784 | tf_op jit(solution)/shard_map/ppermute | solution.py:405
  4.1 0.0 copy-done
  4.1 0.0 copy-done.2
  4.1 0.0 copy-done.1
  4.1 2.9 %front.3 = (bf16[512,128]{1,0:T(8,128)(2,1)S(1)}, bf16[512,128]{1,0:T(8,128)(2,1)S(1)}) custom-call(f32[1]{0:T(128)S(6)} %copy.9.rho, f32[1,32,128,128]{3,2,1,0:T(8,128)S(1)} %copy-done, bf16[1,32,128,128]{3,2,1,0:T(8,128)(2,1)S(1)} %copy-done.1, bf16[1,32,128,128]{3,2,1,0:T(8,128)(2,1)S(1)} %copy-done.2, f32[32,128,128]{2,1,0:T(8,128)} %src.5, ...), custom_call_target="tpu_custom_call" | custom-call | flops 16384000 | bytes 11468800 | tf_op jit(solution)/shard_map/front/pallas_call | solution.py:254
  7.1 5.0 %collective-permute-start.4 = (bf16[512,128]{1,0:T(8,128)(2,1)S(1)}, bf16[512,128]{1,0:T(8,128)(2,1)S(1)}, u32[]{:S(2)}, u32[]{:S(2)}) collective-permute-start(bf16[512,128]{1,0:T(8,128)(2,1)S(1)} %get-tuple-element.25), channel_id=1, source_target_pairs={{0,10},{2,8},{4,14},{6,12},{8,2},{10,0},{12,6},{14,4},{1,11},{3,9}... | collective-permute-start | bytes 393224 | tf_op jit(solution)/shard_map/ppermute | solution.py:400
  12.1 0.3 collective-permute-start.3
  12.4 4.1 %front.4 = (bf16[512,128]{1,0:T(8,128)(2,1)S(1)}, bf16[512,128]{1,0:T(8,128)(2,1)S(1)}, bf16[512,128]{1,0:T(8,128)(2,1)S(1)}, bf16[512,128]{1,0:T(8,128)(2,1)S(1)}) custom-call(f32[1]{0:T(128)S(6)} %copy.9.rho, f32[1,32,128,128]{3,2,1,0:T(8,128)S(1)} %copy-done, bf16[1,32,128,128]{3,2,1,0:T(8,128)(2,1)S(1)} %copy-done.1, ...), custom_call_target="tpu_custom_call" | custom-call | flops 29491200 | bytes 20643840 | tf_op jit(solution)/shard_map/front/pallas_call | solution.py:254
  16.5 0.4 collective-permute-start.5
  16.8 1.8 %collective-permute-start.6 = (bf16[512,128]{1,0:T(8,128)(2,1)S(1)}, bf16[512,128]{1,0:T(8,128)(2,1)S(1)}, u32[]{:S(2)}, u32[]{:S(2)}) collective-permute-start(bf16[512,128]{1,0:T(8,128)(2,1)S(1)} %get-tuple-element.27), channel_id=1, source_target_pairs={{0,4},{2,6},{4,0},{6,2},{8,12},{10,14},{12,8},{14,10},{1,5},{3,7},... | collective-permute-start | bytes 393224 | tf_op jit(solution)/shard_map/ppermute | solution.py:400
  18.6 1.4 %collective-permute-start.7 = (bf16[512,128]{1,0:T(8,128)(2,1)S(1)}, bf16[512,128]{1,0:T(8,128)(2,1)S(1)}, u32[]{:S(2)}, u32[]{:S(2)}) collective-permute-start(bf16[512,128]{1,0:T(8,128)(2,1)S(1)} %get-tuple-element.28), channel_id=1, source_target_pairs={{0,6},{2,4},{4,2},{6,0},{8,14},{10,12},{12,10},{14,8},{1,7},{3,5},... | collective-permute-start | bytes 393224 | tf_op jit(solution)/shard_map/ppermute | solution.py:400
  20.0 0.0 copy-start.3
  20.0 2.9 %front.5 = (bf16[512,128]{1,0:T(8,128)(2,1)S(1)}, bf16[512,128]{1,0:T(8,128)(2,1)S(1)}) custom-call(f32[1]{0:T(128)S(6)} %copy.9.rho, f32[1,32,128,128]{3,2,1,0:T(8,128)S(1)} %copy-done, bf16[1,32,128,128]{3,2,1,0:T(8,128)(2,1)S(1)} %copy-done.1, bf16[1,32,128,128]{3,2,1,0:T(8,128)(2,1)S(1)} %copy-done.2, f32[32,128,128]{2,1,0:T(8,128)} %src.5, ...), custom_call_target="tpu_custom_call" | custom-call | flops 16384000 | bytes 11468800 | tf_op jit(solution)/shard_map/front/pallas_call | solution.py:254
  23.0 0.0 collective-permute-done.4.rest_3_
  23.0 3.7 %collective-permute-start.1 = (bf16[512,128]{1,0:T(8,128)(2,1)S(1)}, bf16[512,128]{1,0:T(8,128)(2,1)S(1)}, u32[]{:S(2)}, u32[]{:S(2)}) collective-permute-start(bf16[512,128]{1,0:T(8,128)(2,1)S(1)} %get-tuple-element.23), channel_id=1, source_target_pairs={{0,12},{2,14},{4,8},{6,10},{8,4},{10,6},{12,0},{14,2},{1,13},{3,15... | collective-permute-start | bytes 393224 | tf_op jit(solution)/shard_map/ppermute | solution.py:400
  26.6 0.0 collective-permute-done.3.rest_2_
  26.6 1.2 %collective-permute-start.2 = (bf16[512,128]{1,0:T(8,128)(2,1)S(1)}, bf16[512,128]{1,0:T(8,128)(2,1)S(1)}, u32[]{:S(2)}, u32[]{:S(2)}) collective-permute-start(bf16[512,128]{1,0:T(8,128)(2,1)S(1)} %get-tuple-element.24), channel_id=1, source_target_pairs={{0,14},{2,12},{4,10},{6,8},{8,6},{10,4},{12,2},{14,0},{1,15},{3,13... | collective-permute-start | bytes 393224 | tf_op jit(solution)/shard_map/ppermute | solution.py:400
  27.9 0.0 collective-permute-done.5.rest_4_
  27.9 2.2 %collective-permute-done.6.rest_5_ = bf16[512,128]{1,0:T(8,128)(2,1)S(1)} collective-permute-done((bf16[512,128]{1,0:T(8,128)(2,1)S(1)}, bf16[512,128]{1,0:T(8,128)(2,1)S(1)}, u32[]{:S(2)}, u32[]{:S(2)}) %collective-permute-start.6) | collective-permute-done | bytes 131104 | tf_op jit(solution)/shard_map/ppermute | solution.py:400
  30.1 5.4 %collective-permute-done.7.rest_6_ = bf16[512,128]{1,0:T(8,128)(2,1)S(1)} collective-permute-done((bf16[512,128]{1,0:T(8,128)(2,1)S(1)}, bf16[512,128]{1,0:T(8,128)(2,1)S(1)}, u32[]{:S(2)}, u32[]{:S(2)}) %collective-permute-start.7) | collective-permute-done | bytes 131104 | tf_op jit(solution)/shard_map/ppermute | solution.py:400
  35.5 0.0 collective-permute-done.1.rest_0_
  35.5 0.0 collective-permute-done.2.rest_1_
  35.5 0.0 copy-done.3
  35.5 1.5 %mix.1 = (bf16[512,128]{1,0:T(8,128)(2,1)S(1)}, bf16[512,128]{1,0:T(8,128)(2,1)S(1)}, bf16[512,128]{1,0:T(8,128)(2,1)S(1)}, bf16[512,128]{1,0:T(8,128)(2,1)S(1)}...) custom-call(f32[8,8]{1,0:T(8,128)S(1)} %copy-done.3, ...), custom_call_target="tpu_custom_call" | custom-call | flops 8388608 | bytes 2097152 | tf_op jit(solution)/shard_map/mix/pallas_call | solution.py:328
  37.0 2.7 %collective-permute-start.8 = (bf16[512,128]{1,0:T(8,128)(2,1)S(1)}, bf16[512,128]{1,0:T(8,128)(2,1)S(1)}, u32[]{:S(2)}, u32[]{:S(2)}) collective-permute-start(bf16[512,128]{1,0:T(8,128)(2,1)S(1)} %get-tuple-element.29), channel_id=1, source_target_pairs={{0,8},{2,10},{4,12},{6,14},{8,0},{10,2},{12,4},{14,6},{1,9},{3,11}... | collective-permute-start | bytes 393224 | tf_op jit(solution)/shard_map/ppermute | solution.py:400
  39.7 1.5 %collective-permute-start.9 = (bf16[512,128]{1,0:T(8,128)(2,1)S(1)}, bf16[512,128]{1,0:T(8,128)(2,1)S(1)}, u32[]{:S(2)}, u32[]{:S(2)}) collective-permute-start(bf16[512,128]{1,0:T(8,128)(2,1)S(1)} %get-tuple-element.30), channel_id=1, source_target_pairs={{0,2},{2,0},{4,6},{6,4},{8,10},{10,8},{12,14},{14,12},{1,3},{3,1},... | collective-permute-start | bytes 393224 | tf_op jit(solution)/shard_map/ppermute | solution.py:400
  41.2 0.3 collective-permute-start.10
  41.4 3.5 %collective-permute-start.11 = (bf16[512,128]{1,0:T(8,128)(2,1)S(1)}, bf16[512,128]{1,0:T(8,128)(2,1)S(1)}, u32[]{:S(2)}, u32[]{:S(2)}) collective-permute-start(bf16[512,128]{1,0:T(8,128)(2,1)S(1)} %get-tuple-element.32), channel_id=1, source_target_pairs={{0,12},{2,14},{4,8},{6,10},{8,4},{10,6},{12,0},{14,2},{1,13},{3,15... | collective-permute-start | bytes 393224 | tf_op jit(solution)/shard_map/ppermute | solution.py:400
  44.9 1.1 %collective-permute-start.12 = (bf16[512,128]{1,0:T(8,128)(2,1)S(1)}, bf16[512,128]{1,0:T(8,128)(2,1)S(1)}, u32[]{:S(2)}, u32[]{:S(2)}) collective-permute-start(bf16[512,128]{1,0:T(8,128)(2,1)S(1)} %get-tuple-element.33), channel_id=1, source_target_pairs={{0,14},{2,12},{4,10},{6,8},{8,6},{10,4},{12,2},{14,0},{1,15},{3,13... | collective-permute-start | bytes 393224 | tf_op jit(solution)/shard_map/ppermute | solution.py:400
  46.0 9.5 %collective-permute-done.8.rest_0_ = bf16[512,128]{1,0:T(8,128)(2,1)S(1)} collective-permute-done((bf16[512,128]{1,0:T(8,128)(2,1)S(1)}, bf16[512,128]{1,0:T(8,128)(2,1)S(1)}, u32[]{:S(2)}, u32[]{:S(2)}) %collective-permute-start.8) | collective-permute-done | bytes 131104 | tf_op jit(solution)/shard_map/ppermute | solution.py:400
  55.5 0.0 collective-permute-start.13
  55.5 0.0 collective-permute-done.9.rest_1_
  55.5 2.4 %collective-permute-start.14 = (bf16[512,128]{1,0:T(8,128)(2,1)S(1)}, bf16[512,128]{1,0:T(8,128)(2,1)S(1)}, u32[]{:S(2)}, u32[]{:S(2)}) collective-permute-start(bf16[512,128]{1,0:T(8,128)(2,1)S(1)} %get-tuple-element.35), channel_id=1, source_target_pairs={{0,6},{2,4},{4,2},{6,0},{8,14},{10,12},{12,10},{14,8},{1,7},{3,5},... | collective-permute-start | bytes 393224 | tf_op jit(solution)/shard_map/ppermute | solution.py:400
  58.0 0.8 %collective-permute-done.10.rest_2_ = bf16[512,128]{1,0:T(8,128)(2,1)S(1)} collective-permute-done((bf16[512,128]{1,0:T(8,128)(2,1)S(1)}, bf16[512,128]{1,0:T(8,128)(2,1)S(1)}, u32[]{:S(2)}, u32[]{:S(2)}) %collective-permute-start.10) | collective-permute-done | bytes 131104 | tf_op jit(solution)/shard_map/ppermute | solution.py:400
  58.7 0.0 collective-permute-done.11.rest_3_
  58.7 0.0 collective-permute-done.12.rest_4_
  58.7 2.9 %collective-permute-done.13.rest_5_ = bf16[512,128]{1,0:T(8,128)(2,1)S(1)} collective-permute-done((bf16[512,128]{1,0:T(8,128)(2,1)S(1)}, bf16[512,128]{1,0:T(8,128)(2,1)S(1)}, u32[]{:S(2)}, u32[]{:S(2)}) %collective-permute-start.13) | collective-permute-done | bytes 131104 | tf_op jit(solution)/shard_map/ppermute | solution.py:400
  61.6 1.6 %collective-permute-done.14.rest_6_ = bf16[512,128]{1,0:T(8,128)(2,1)S(1)} collective-permute-done((bf16[512,128]{1,0:T(8,128)(2,1)S(1)}, bf16[512,128]{1,0:T(8,128)(2,1)S(1)}, u32[]{:S(2)}, u32[]{:S(2)}) %collective-permute-start.14) | collective-permute-done | bytes 131104 | tf_op jit(solution)/shard_map/ppermute | solution.py:400
  63.2 1.7 %last.1 = f32[1,32,128,128]{3,2,1,0:T(8,128)} custom-call(f32[1]{0:T(128)S(6)} %copy.9.rho, f32[8,8]{1,0:T(8,128)S(1)} %copy-done.3, f32[1,32,128,128]{3,2,1,0:T(8,128)S(1)} %copy-done, bf16[512,128]{1,0:T(8,128)(2,1)S(1)} %collective-permute-done.8.rest_0_, bf16[512,128]{1,0:T(8,128)(2,1)S(1)} %collective-permute-done.9.rest_1_, ...), custom_call_target="tpu_custom_call" | custom-call | flops 2097152 | bytes 5242880 | tf_op jit(solution)/shard_map/last/pallas_call | solution.py:379
Async XLA Ops:
  0.0 4.1 %copy-start = (f32[1,32,128,128]{3,2,1,0:T(8,128)S(1)}, f32[1,32,128,128]{3,2,1,0:T(8,128)}, u32[]{:S(2)}) copy-start(f32[1,32,128,128]{3,2,1,0:T(8,128)} %p.7) | copy-start | bytes 6291460
  0.0 4.1 %copy-start.2 = (bf16[1,32,128,128]{3,2,1,0:T(8,128)(2,1)S(1)}, bf16[1,32,128,128]{3,2,1,0:T(8,128)(2,1)}, u32[]{:S(2)}) copy-start(bf16[1,32,128,128]{3,2,1,0:T(8,128)(2,1)} %s1_.5) | copy-start | bytes 3145732
  0.0 4.1 %copy-start.1 = (bf16[1,32,128,128]{3,2,1,0:T(8,128)(2,1)S(1)}, bf16[1,32,128,128]{3,2,1,0:T(8,128)(2,1)}, u32[]{:S(2)}) copy-start(bf16[1,32,128,128]{3,2,1,0:T(8,128)(2,1)} %s0.5) | copy-start | bytes 3145732
  1.9 2.2 %collective-permute-start = (f32[7,128,128]{2,1,0:T(8,128)}, f32[7,128,128]{2,1,0:T(8,128)S(1)}, u32[]{:S(2)}, u32[]{:S(2)}) collective-permute-start(f32[7,128,128]{2,1,0:T(8,128)} %pack.1), channel_id=1, source_target_pairs={{0,1},{1,0},{2,3},{3,2},{4,5},{5,4},{6,7},{7,6},{8,9},{9,8},{10,11... | collective-permute-start | bytes 1376264 | tf_op jit(solution)/shard_map/ppermute | solution.py:405
  7.1 15.9 %collective-permute-start.4 = (bf16[512,128]{1,0:T(8,128)(2,1)S(1)}, bf16[512,128]{1,0:T(8,128)(2,1)S(1)}, u32[]{:S(2)}, u32[]{:S(2)}) collective-permute-start(bf16[512,128]{1,0:T(8,128)(2,1)S(1)} %get-tuple-element.25), channel_id=1, source_target_pairs={{0,10},{2,8},{4,14},{6,12},{8,2},{10,0},{12,6},{14,4},{1,11},{3,9}... | collective-permute-start | bytes 393224 | tf_op jit(solution)/shard_map/ppermute | solution.py:400
  12.1 14.6 %collective-permute-start.3 = (bf16[512,128]{1,0:T(8,128)(2,1)S(1)}, bf16[512,128]{1,0:T(8,128)(2,1)S(1)}, u32[]{:S(2)}, u32[]{:S(2)}) collective-permute-start(bf16[512,128]{1,0:T(8,128)(2,1)S(1)} %get-tuple-element.21.rest_0_), channel_id=1, source_target_pairs={{0,8},{2,10},{4,12},{6,14},{8,0},{10,2},{12,4},{14,6},{1,9},{3,11}... | collective-permute-start | bytes 393224 | tf_op jit(solution)/shard_map/ppermute | solution.py:400
  16.5 11.4 %collective-permute-start.5 = (bf16[512,128]{1,0:T(8,128)(2,1)S(1)}, bf16[512,128]{1,0:T(8,128)(2,1)S(1)}, u32[]{:S(2)}, u32[]{:S(2)}) collective-permute-start(bf16[512,128]{1,0:T(8,128)(2,1)S(1)} %get-tuple-element.26), channel_id=1, source_target_pairs={{0,2},{2,0},{4,6},{6,4},{8,10},{10,8},{12,14},{14,12},{1,3},{3,1},... | collective-permute-start | bytes 393224 | tf_op jit(solution)/shard_map/ppermute | solution.py:400
  16.8 13.3 %collective-permute-start.6 = (bf16[512,128]{1,0:T(8,128)(2,1)S(1)}, bf16[512,128]{1,0:T(8,128)(2,1)S(1)}, u32[]{:S(2)}, u32[]{:S(2)}) collective-permute-start(bf16[512,128]{1,0:T(8,128)(2,1)S(1)} %get-tuple-element.27), channel_id=1, source_target_pairs={{0,4},{2,6},{4,0},{6,2},{8,12},{10,14},{12,8},{14,10},{1,5},{3,7},... | collective-permute-start | bytes 393224 | tf_op jit(solution)/shard_map/ppermute | solution.py:400
  18.6 16.9 %collective-permute-start.7 = (bf16[512,128]{1,0:T(8,128)(2,1)S(1)}, bf16[512,128]{1,0:T(8,128)(2,1)S(1)}, u32[]{:S(2)}, u32[]{:S(2)}) collective-permute-start(bf16[512,128]{1,0:T(8,128)(2,1)S(1)} %get-tuple-element.28), channel_id=1, source_target_pairs={{0,6},{2,4},{4,2},{6,0},{8,14},{10,12},{12,10},{14,8},{1,7},{3,5},... | collective-permute-start | bytes 393224 | tf_op jit(solution)/shard_map/ppermute | solution.py:400
  20.0 15.5 %copy-start.3 = (f32[8,8]{1,0:T(8,128)S(1)}, f32[8,8]{1,0:T(8,128)}, u32[]{:S(2)}) copy-start(f32[8,8]{1,0:T(8,128)} %weights.3) | copy-start | bytes 772
  23.0 12.5 %collective-permute-start.1 = (bf16[512,128]{1,0:T(8,128)(2,1)S(1)}, bf16[512,128]{1,0:T(8,128)(2,1)S(1)}, u32[]{:S(2)}, u32[]{:S(2)}) collective-permute-start(bf16[512,128]{1,0:T(8,128)(2,1)S(1)} %get-tuple-element.23), channel_id=1, source_target_pairs={{0,12},{2,14},{4,8},{6,10},{8,4},{10,6},{12,0},{14,2},{1,13},{3,15... | collective-permute-start | bytes 393224 | tf_op jit(solution)/shard_map/ppermute | solution.py:400
  26.6 8.9 %collective-permute-start.2 = (bf16[512,128]{1,0:T(8,128)(2,1)S(1)}, bf16[512,128]{1,0:T(8,128)(2,1)S(1)}, u32[]{:S(2)}, u32[]{:S(2)}) collective-permute-start(bf16[512,128]{1,0:T(8,128)(2,1)S(1)} %get-tuple-element.24), channel_id=1, source_target_pairs={{0,14},{2,12},{4,10},{6,8},{8,6},{10,4},{12,2},{14,0},{1,15},{3,13... | collective-permute-start | bytes 393224 | tf_op jit(solution)/shard_map/ppermute | solution.py:400
  37.0 18.5 %collective-permute-start.8 = (bf16[512,128]{1,0:T(8,128)(2,1)S(1)}, bf16[512,128]{1,0:T(8,128)(2,1)S(1)}, u32[]{:S(2)}, u32[]{:S(2)}) collective-permute-start(bf16[512,128]{1,0:T(8,128)(2,1)S(1)} %get-tuple-element.29), channel_id=1, source_target_pairs={{0,8},{2,10},{4,12},{6,14},{8,0},{10,2},{12,4},{14,6},{1,9},{3,11}... | collective-permute-start | bytes 393224 | tf_op jit(solution)/shard_map/ppermute | solution.py:400
  39.7 15.9 %collective-permute-start.9 = (bf16[512,128]{1,0:T(8,128)(2,1)S(1)}, bf16[512,128]{1,0:T(8,128)(2,1)S(1)}, u32[]{:S(2)}, u32[]{:S(2)}) collective-permute-start(bf16[512,128]{1,0:T(8,128)(2,1)S(1)} %get-tuple-element.30), channel_id=1, source_target_pairs={{0,2},{2,0},{4,6},{6,4},{8,10},{10,8},{12,14},{14,12},{1,3},{3,1},... | collective-permute-start | bytes 393224 | tf_op jit(solution)/shard_map/ppermute | solution.py:400
  41.2 17.5 %collective-permute-start.10 = (bf16[512,128]{1,0:T(8,128)(2,1)S(1)}, bf16[512,128]{1,0:T(8,128)(2,1)S(1)}, u32[]{:S(2)}, u32[]{:S(2)}) collective-permute-start(bf16[512,128]{1,0:T(8,128)(2,1)S(1)} %get-tuple-element.31), channel_id=1, source_target_pairs={{0,10},{2,8},{4,14},{6,12},{8,2},{10,0},{12,6},{14,4},{1,11},{3,9}... | collective-permute-start | bytes 393224 | tf_op jit(solution)/shard_map/ppermute | solution.py:400
  41.4 17.3 %collective-permute-start.11 = (bf16[512,128]{1,0:T(8,128)(2,1)S(1)}, bf16[512,128]{1,0:T(8,128)(2,1)S(1)}, u32[]{:S(2)}, u32[]{:S(2)}) collective-permute-start(bf16[512,128]{1,0:T(8,128)(2,1)S(1)} %get-tuple-element.32), channel_id=1, source_target_pairs={{0,12},{2,14},{4,8},{6,10},{8,4},{10,6},{12,0},{14,2},{1,13},{3,15... | collective-permute-start | bytes 393224 | tf_op jit(solution)/shard_map/ppermute | solution.py:400
  44.9 13.8 %collective-permute-start.12 = (bf16[512,128]{1,0:T(8,128)(2,1)S(1)}, bf16[512,128]{1,0:T(8,128)(2,1)S(1)}, u32[]{:S(2)}, u32[]{:S(2)}) collective-permute-start(bf16[512,128]{1,0:T(8,128)(2,1)S(1)} %get-tuple-element.33), channel_id=1, source_target_pairs={{0,14},{2,12},{4,10},{6,8},{8,6},{10,4},{12,2},{14,0},{1,15},{3,13... | collective-permute-start | bytes 393224 | tf_op jit(solution)/shard_map/ppermute | solution.py:400
  55.5 6.1 %collective-permute-start.13 = (bf16[512,128]{1,0:T(8,128)(2,1)S(1)}, bf16[512,128]{1,0:T(8,128)(2,1)S(1)}, u32[]{:S(2)}, u32[]{:S(2)}) collective-permute-start(bf16[512,128]{1,0:T(8,128)(2,1)S(1)} %get-tuple-element.34), channel_id=1, source_target_pairs={{0,4},{2,6},{4,0},{6,2},{8,12},{10,14},{12,8},{14,10},{1,5},{3,7},... | collective-permute-start | bytes 393224 | tf_op jit(solution)/shard_map/ppermute | solution.py:400
  55.5 7.7 %collective-permute-start.14 = (bf16[512,128]{1,0:T(8,128)(2,1)S(1)}, bf16[512,128]{1,0:T(8,128)(2,1)S(1)}, u32[]{:S(2)}, u32[]{:S(2)}) collective-permute-start(bf16[512,128]{1,0:T(8,128)(2,1)S(1)} %get-tuple-element.35), channel_id=1, source_target_pairs={{0,6},{2,4},{4,2},{6,0},{8,14},{10,12},{12,10},{14,8},{1,7},{3,5},... | collective-permute-start | bytes 393224 | tf_op jit(solution)/shard_map/ppermute | solution.py:400

commit v4 on v3

--- a/solution.py
+++ b/solution.py
@@ -394,7 +394,7 @@
     parts = kernel.shape[0]
     arrays = (particles, state_zero, state_one, source, observed, absorb)
     far, near = tuple(range(parts // 2, parts)), tuple(range(1, parts // 2))
-    order = (far[0], *near[:1], *far[1:], *near[1:], 0)
+    order = (far[0], *near[:2], *far[1:], *near[2:], 0)
 
     def hop(value, s):
         return lax.ppermute(value, "dom", [(i, i ^ s) for i in range(parts)])
@@ -413,7 +413,10 @@
     got = hops(fields, lead)
     got = dict(zip(order, mix(kernel, got, lead, order)))
     got = dict(zip(order, hops(got, order)))
-    return last(inv_width, kernel, particles, [got[s] for s in order], 0, layers, order, None)
+    result = None
+    for steps in ((*order[:3], 0), order[3:-1]):
+        result = last(inv_width, kernel, particles, [got[s] for s in steps], 0, layers, steps, result)
+    return result
 
 
 def solution(mesh):

time: 65.1 us -> 62.9 us (0.966)
  waiting for transfers between devices: 23.5 us -> 19 us
  starting transfers between devices: 25.7 us -> 27 us
  Pallas kernels: 15 us -> 16 us
    ppermute x14, waiting for transfers between devices: 22.5 us -> 18 us  [hop(): return lax.ppermute(value, 'dom', [(i, i ^ s) for i in range(parts)])]
    ppermute x14, starting transfers between devices: 25.2 us -> 26.5 us  [hop(): return lax.ppermute(value, 'dom', [(i, i ^ s) for i in range(parts)])]
    pallas_call x1 -> x2, Pallas kernels: 1.67 us -> 2.39 us  [last(): pl.pallas_call(functools.partial(last_kernel, geometry), out_shape=jax.Sh...]
  transfers between devices with their start and end apart: 15 -> 15, of which waited for: 7 -> 6; matrix products, arithmetic and copies ran while one was open for 0% -> 0% of each run, Pallas kernels for 11% -> 13%
where the time goes in v4:
time: 62.9 us; the launch traced here: 62.7 us
  starting transfers between devices  27 us (43%)
  waiting for transfers between devices  19 us (30%)
  Pallas kernels  16 us (25%)
  between operations  0.73 us (1%)
    ppermute x14, starting transfers between devices, hop(): return lax.ppermute(value, 'dom', [(i, i ^ s) for i in range(parts)])  26.5 us
    ppermute x14, waiting for transfers between devices, hop(): return lax.ppermute(value, 'dom', [(i, i ^ s) for i in range(parts)])  18 us
    pallas_call x3, Pallas kernels, front(): pl.pallas_call(functools.partial(front_kernel, geometry), out_shape=[jax....  10.2 us
    pallas_call x2, Pallas kernels, last(): pl.pallas_call(functools.partial(last_kernel, geometry), out_shape=jax.Sh...  2.39 us
    pallas_call x1, Pallas kernels, pack(): pl.pallas_call(pack_kernel, out_shape=jax.ShapeDtypeStruct((7, nx, ny), f...  1.93 us
    pallas_call x1, Pallas kernels, mix(): pl.pallas_call(functools.partial(mix_kernel, parts, steps, members), out_...  1.46 us
  transfers between devices with their start and end apart: 15, of which 6 were waited for; matrix products, arithmetic and copies ran while one was open for 0% of the time, Pallas kernels for 13%

profile of v4, /device:TPU:0, one launch (start us, length us, event | category | flops | bytes accessed | tf_op | source)
XLA Modules:
  0.0 62.7 jit_solution(16548038969307713626)
XLA Ops:
  0.0 0.0 copy-start
  0.0 0.0 copy-start.2
  0.0 0.0 copy-start.1
  0.0 1.9 %pack.1 = f32[7,128,128]{2,1,0:T(8,128)} custom-call(f32[1,32,128,128]{3,2,1,0:T(8,128)} %p.9, bf16[1,32,128,128]{3,2,1,0:T(8,128)(2,1)} %s0.5, bf16[1,32,128,128]{3,2,1,0:T(8,128)(2,1)} %s1_.5, f32[32,128,128]{2,1,0:T(8,128)} %src.5, f32[32,128,128]{2,1,0:T(8,128)} %obs.5, f32[32,128,128]{2,1,0:T(8,128)} %ab.5), custom_call_target="tpu_custom_call" | custom-call | tf_op jit(solution)/shard_map/pack/pallas_call | solution.py:56
  1.9 0.5 collective-permute-start
  3.1 1.0 %collective-permute-done.halo = f32[7,128,128]{2,1,0:T(8,128)S(1)} collective-permute-done((f32[7,128,128]{2,1,0:T(8,128)}, f32[7,128,128]{2,1,0:T(8,128)S(1)}, u32[]{:S(2)}, u32[]{:S(2)}) %collective-permute-start) | collective-permute-done | bytes 458784 | tf_op jit(solution)/shard_map/ppermute | solution.py:405
  4.1 0.0 copy-done
  4.1 0.0 copy-done.2
  4.1 0.0 copy-done.1
  4.1 3.0 %front.3 = (bf16[512,128]{1,0:T(8,128)(2,1)S(1)}, bf16[512,128]{1,0:T(8,128)(2,1)S(1)}) custom-call(f32[1]{0:T(128)S(6)} %copy.11.rho, f32[1,32,128,128]{3,2,1,0:T(8,128)S(1)} %copy-done, bf16[1,32,128,128]{3,2,1,0:T(8,128)(2,1)S(1)} %copy-done.1, bf16[1,32,128,128]{3,2,1,0:T(8,128)(2,1)S(1)} %copy-done.2, f32[32,128,128]{2,1,0:T(8,128)} %src.5, ...), custom_call_target="tpu_custom_call" | custom-call | flops 16384000 | bytes 11468800 | tf_op jit(solution)/shard_map/front/pallas_call | solution.py:254
  7.1 5.0 %collective-permute-start.4 = (bf16[512,128]{1,0:T(8,128)(2,1)S(1)}, bf16[512,128]{1,0:T(8,128)(2,1)S(1)}, u32[]{:S(2)}, u32[]{:S(2)}) collective-permute-start(bf16[512,128]{1,0:T(8,128)(2,1)S(1)} %get-tuple-element.25), channel_id=1, source_target_pairs={{0,10},{2,8},{4,14},{6,12},{8,2},{10,0},{12,6},{14,4},{1,11},{3,9}... | collective-permute-start | bytes 393224 | tf_op jit(solution)/shard_map/ppermute | solution.py:400
  12.1 0.3 collective-permute-start.3
  12.5 4.2 %front.4 = (bf16[512,128]{1,0:T(8,128)(2,1)S(1)}, bf16[512,128]{1,0:T(8,128)(2,1)S(1)}, bf16[512,128]{1,0:T(8,128)(2,1)S(1)}, bf16[512,128]{1,0:T(8,128)(2,1)S(1)}) custom-call(f32[1]{0:T(128)S(6)} %copy.11.rho, f32[1,32,128,128]{3,2,1,0:T(8,128)S(1)} %copy-done, bf16[1,32,128,128]{3,2,1,0:T(8,128)(2,1)S(1)} %copy-done.1, ...), custom_call_target="tpu_custom_call" | custom-call | flops 29491200 | bytes 20643840 | tf_op jit(solution)/shard_map/front/pallas_call | solution.py:254
  16.7 0.4 collective-permute-start.5
  17.1 1.8 %collective-permute-start.6 = (bf16[512,128]{1,0:T(8,128)(2,1)S(1)}, bf16[512,128]{1,0:T(8,128)(2,1)S(1)}, u32[]{:S(2)}, u32[]{:S(2)}) collective-permute-start(bf16[512,128]{1,0:T(8,128)(2,1)S(1)} %get-tuple-element.27), channel_id=1, source_target_pairs={{0,4},{2,6},{4,0},{6,2},{8,12},{10,14},{12,8},{14,10},{1,5},{3,7},... | collective-permute-start | bytes 393224 | tf_op jit(solution)/shard_map/ppermute | solution.py:400
  18.8 1.4 %collective-permute-start.7 = (bf16[512,128]{1,0:T(8,128)(2,1)S(1)}, bf16[512,128]{1,0:T(8,128)(2,1)S(1)}, u32[]{:S(2)}, u32[]{:S(2)}) collective-permute-start(bf16[512,128]{1,0:T(8,128)(2,1)S(1)} %get-tuple-element.28), channel_id=1, source_target_pairs={{0,6},{2,4},{4,2},{6,0},{8,14},{10,12},{12,10},{14,8},{1,7},{3,5},... | collective-permute-start | bytes 393224 | tf_op jit(solution)/shard_map/ppermute | solution.py:400
  20.2 0.0 copy-start.3
  20.2 3.0 %front.5 = (bf16[512,128]{1,0:T(8,128)(2,1)S(1)}, bf16[512,128]{1,0:T(8,128)(2,1)S(1)}) custom-call(f32[1]{0:T(128)S(6)} %copy.11.rho, f32[1,32,128,128]{3,2,1,0:T(8,128)S(1)} %copy-done, bf16[1,32,128,128]{3,2,1,0:T(8,128)(2,1)S(1)} %copy-done.1, bf16[1,32,128,128]{3,2,1,0:T(8,128)(2,1)S(1)} %copy-done.2, f32[32,128,128]{2,1,0:T(8,128)} %src.5, ...), custom_call_target="tpu_custom_call" | custom-call | flops 16384000 | bytes 11468800 | tf_op jit(solution)/shard_map/front/pallas_call | solution.py:254
  23.2 0.0 collective-permute-done.4.rest_3_
  23.2 3.7 %collective-permute-start.1 = (bf16[512,128]{1,0:T(8,128)(2,1)S(1)}, bf16[512,128]{1,0:T(8,128)(2,1)S(1)}, u32[]{:S(2)}, u32[]{:S(2)}) collective-permute-start(bf16[512,128]{1,0:T(8,128)(2,1)S(1)} %get-tuple-element.23), channel_id=1, source_target_pairs={{0,12},{2,14},{4,8},{6,10},{8,4},{10,6},{12,0},{14,2},{1,13},{3,15... | collective-permute-start | bytes 393224 | tf_op jit(solution)/shard_map/ppermute | solution.py:400
  26.9 0.0 collective-permute-done.3.rest_2_
  26.9 1.0 %collective-permute-start.2 = (bf16[512,128]{1,0:T(8,128)(2,1)S(1)}, bf16[512,128]{1,0:T(8,128)(2,1)S(1)}, u32[]{:S(2)}, u32[]{:S(2)}) collective-permute-start(bf16[512,128]{1,0:T(8,128)(2,1)S(1)} %get-tuple-element.24), channel_id=1, source_target_pairs={{0,14},{2,12},{4,10},{6,8},{8,6},{10,4},{12,2},{14,0},{1,15},{3,13... | collective-permute-start | bytes 393224 | tf_op jit(solution)/shard_map/ppermute | solution.py:400
  27.9 0.0 collective-permute-done.5.rest_4_
  27.9 2.2 %collective-permute-done.6.rest_5_ = bf16[512,128]{1,0:T(8,128)(2,1)S(1)} collective-permute-done((bf16[512,128]{1,0:T(8,128)(2,1)S(1)}, bf16[512,128]{1,0:T(8,128)(2,1)S(1)}, u32[]{:S(2)}, u32[]{:S(2)}) %collective-permute-start.6) | collective-permute-done | bytes 131104 | tf_op jit(solution)/shard_map/ppermute | solution.py:400
  30.2 5.4 %collective-permute-done.7.rest_6_ = bf16[512,128]{1,0:T(8,128)(2,1)S(1)} collective-permute-done((bf16[512,128]{1,0:T(8,128)(2,1)S(1)}, bf16[512,128]{1,0:T(8,128)(2,1)S(1)}, u32[]{:S(2)}, u32[]{:S(2)}) %collective-permute-start.7) | collective-permute-done | bytes 131104 | tf_op jit(solution)/shard_map/ppermute | solution.py:400
  35.6 0.0 collective-permute-done.1.rest_0_
  35.6 0.0 collective-permute-done.2.rest_1_
  35.6 0.0 copy-done.3
  35.6 1.5 %mix.1 = (bf16[512,128]{1,0:T(8,128)(2,1)S(1)}, bf16[512,128]{1,0:T(8,128)(2,1)S(1)}, bf16[512,128]{1,0:T(8,128)(2,1)S(1)}, bf16[512,128]{1,0:T(8,128)(2,1)S(1)}...) custom-call(f32[8,8]{1,0:T(8,128)S(1)} %copy-done.3, ...), custom_call_target="tpu_custom_call" | custom-call | flops 8388608 | bytes 2097152 | tf_op jit(solution)/shard_map/mix/pallas_call | solution.py:328
  37.1 2.9 %collective-permute-start.12 = (bf16[512,128]{1,0:T(8,128)(2,1)S(1)}, bf16[512,128]{1,0:T(8,128)(2,1)S(1)}, u32[]{:S(2)}, u32[]{:S(2)}) collective-permute-start(bf16[512,128]{1,0:T(8,128)(2,1)S(1)} %get-tuple-element.33), channel_id=1, source_target_pairs={{0,8},{2,10},{4,12},{6,14},{8,0},{10,2},{12,4},{14,6},{1,9},{3,11}... | collective-permute-start | bytes 393224 | tf_op jit(solution)/shard_map/ppermute | solution.py:400
  39.9 1.5 %collective-permute-start.13 = (bf16[512,128]{1,0:T(8,128)(2,1)S(1)}, bf16[512,128]{1,0:T(8,128)(2,1)S(1)}, u32[]{:S(2)}, u32[]{:S(2)}) collective-permute-start(bf16[512,128]{1,0:T(8,128)(2,1)S(1)} %get-tuple-element.34), channel_id=1, source_target_pairs={{0,2},{2,0},{4,6},{6,4},{8,10},{10,8},{12,14},{14,12},{1,3},{3,1},... | collective-permute-start | bytes 393224 | tf_op jit(solution)/shard_map/ppermute | solution.py:400
  41.5 0.0 collective-permute-start.8
  41.5 2.2 %collective-permute-start.14 = (bf16[512,128]{1,0:T(8,128)(2,1)S(1)}, bf16[512,128]{1,0:T(8,128)(2,1)S(1)}, u32[]{:S(2)}, u32[]{:S(2)}) collective-permute-start(bf16[512,128]{1,0:T(8,128)(2,1)S(1)} %get-tuple-element.35), channel_id=1, source_target_pairs={{0,4},{2,6},{4,0},{6,2},{8,12},{10,14},{12,8},{14,10},{1,5},{3,7},... | collective-permute-start | bytes 393224 | tf_op jit(solution)/shard_map/ppermute | solution.py:400
  43.7 2.1 %collective-permute-start.9 = (bf16[512,128]{1,0:T(8,128)(2,1)S(1)}, bf16[512,128]{1,0:T(8,128)(2,1)S(1)}, u32[]{:S(2)}, u32[]{:S(2)}) collective-permute-start(bf16[512,128]{1,0:T(8,128)(2,1)S(1)} %get-tuple-element.30), channel_id=1, source_target_pairs={{0,12},{2,14},{4,8},{6,10},{8,4},{10,6},{12,0},{14,2},{1,13},{3,15... | collective-permute-start | bytes 393224 | tf_op jit(solution)/shard_map/ppermute | solution.py:400
  45.8 5.1 %collective-permute-done.12.rest_0_ = bf16[512,128]{1,0:T(8,128)(2,1)S(1)} collective-permute-done((bf16[512,128]{1,0:T(8,128)(2,1)S(1)}, bf16[512,128]{1,0:T(8,128)(2,1)S(1)}, u32[]{:S(2)}, u32[]{:S(2)}) %collective-permute-start.12) | collective-permute-done | bytes 131104 | tf_op jit(solution)/shard_map/ppermute | solution.py:400
  50.9 4.2 %collective-permute-start.10 = (bf16[512,128]{1,0:T(8,128)(2,1)S(1)}, bf16[512,128]{1,0:T(8,128)(2,1)S(1)}, u32[]{:S(2)}, u32[]{:S(2)}) collective-permute-start(bf16[512,128]{1,0:T(8,128)(2,1)S(1)} %get-tuple-element.31), channel_id=1, source_target_pairs={{0,14},{2,12},{4,10},{6,8},{8,6},{10,4},{12,2},{14,0},{1,15},{3,13... | collective-permute-start | bytes 393224 | tf_op jit(solution)/shard_map/ppermute | solution.py:400
  55.1 0.0 collective-permute-done.13.rest_1_
  55.1 0.0 collective-permute-start.11
  55.1 0.0 collective-permute-done.14.rest_2_
  55.1 1.2 %last.2.rest_4_ = f32[1,32,128,128]{3,2,1,0:T(8,128)} custom-call(f32[1]{0:T(128)S(6)} %copy.11.rho, f32[8,8]{1,0:T(8,128)S(1)} %copy-done.3, f32[1,32,128,128]{3,2,1,0:T(8,128)S(1)} %copy-done, bf16[512,128]{1,0:T(8,128)(2,1)S(1)} %collective-permute-done.12.rest_0_, bf16[512,128]{1,0:T(8,128)(2,1)S(1)} %collective-permute-done.13.rest_1_, ...), custom_call_target="tpu_custom_call" | custom-call | flops 1048576 | bytes 2621440 | tf_op jit(solution)/shard_map/last/pallas_call | solution.py:379
  56.3 2.9 %collective-permute-done.8.rest_0_ = bf16[512,128]{1,0:T(8,128)(2,1)S(1)} collective-permute-done((bf16[512,128]{1,0:T(8,128)(2,1)S(1)}, bf16[512,128]{1,0:T(8,128)(2,1)S(1)}, u32[]{:S(2)}, u32[]{:S(2)}) %collective-permute-start.8) | collective-permute-done | bytes 131104 | tf_op jit(solution)/shard_map/ppermute | solution.py:400
  59.2 0.0 collective-permute-done.9.rest_1_
  59.2 0.0 collective-permute-done.10.rest_2_
  59.2 2.3 %collective-permute-done.11.rest_3_ = bf16[512,128]{1,0:T(8,128)(2,1)S(1)} collective-permute-done((bf16[512,128]{1,0:T(8,128)(2,1)S(1)}, bf16[512,128]{1,0:T(8,128)(2,1)S(1)}, u32[]{:S(2)}, u32[]{:S(2)}) %collective-permute-start.11) | collective-permute-done | bytes 131104 | tf_op jit(solution)/shard_map/ppermute | solution.py:400
  61.5 1.2 %last.3 = f32[1,32,128,128]{3,2,1,0:T(8,128)} custom-call(f32[1]{0:T(128)S(6)} %copy.11.rho, f32[8,8]{1,0:T(8,128)S(1)} %copy-done.3, f32[1,32,128,128]{3,2,1,0:T(8,128)S(1)} %copy-done, bf16[512,128]{1,0:T(8,128)(2,1)S(1)} %collective-permute-done.8.rest_0_, bf16[512,128]{1,0:T(8,128)(2,1)S(1)} %collective-permute-done.9.rest_1_, ...), custom_call_target="tpu_custom_call", output_to_operand_aliasing={{}: (7, {})} | custom-call | flops 1048576 | bytes 2621440 | tf_op jit(solution)/shard_map/last/pallas_call | solution.py:379
Async XLA Ops:
  0.0 4.1 %copy-start = (f32[1,32,128,128]{3,2,1,0:T(8,128)S(1)}, f32[1,32,128,128]{3,2,1,0:T(8,128)}, u32[]{:S(2)}) copy-start(f32[1,32,128,128]{3,2,1,0:T(8,128)} %p.9) | copy-start | bytes 6291460
  0.0 4.1 %copy-start.2 = (bf16[1,32,128,128]{3,2,1,0:T(8,128)(2,1)S(1)}, bf16[1,32,128,128]{3,2,1,0:T(8,128)(2,1)}, u32[]{:S(2)}) copy-start(bf16[1,32,128,128]{3,2,1,0:T(8,128)(2,1)} %s1_.5) | copy-start | bytes 3145732
  0.0 4.1 %copy-start.1 = (bf16[1,32,128,128]{3,2,1,0:T(8,128)(2,1)S(1)}, bf16[1,32,128,128]{3,2,1,0:T(8,128)(2,1)}, u32[]{:S(2)}) copy-start(bf16[1,32,128,128]{3,2,1,0:T(8,128)(2,1)} %s0.5) | copy-start | bytes 3145732
  1.9 2.2 %collective-permute-start = (f32[7,128,128]{2,1,0:T(8,128)}, f32[7,128,128]{2,1,0:T(8,128)S(1)}, u32[]{:S(2)}, u32[]{:S(2)}) collective-permute-start(f32[7,128,128]{2,1,0:T(8,128)} %pack.1), channel_id=1, source_target_pairs={{0,1},{1,0},{2,3},{3,2},{4,5},{5,4},{6,7},{7,6},{8,9},{9,8},{10,11... | collective-permute-start | bytes 1376264 | tf_op jit(solution)/shard_map/ppermute | solution.py:405
  7.1 16.1 %collective-permute-start.4 = (bf16[512,128]{1,0:T(8,128)(2,1)S(1)}, bf16[512,128]{1,0:T(8,128)(2,1)S(1)}, u32[]{:S(2)}, u32[]{:S(2)}) collective-permute-start(bf16[512,128]{1,0:T(8,128)(2,1)S(1)} %get-tuple-element.25), channel_id=1, source_target_pairs={{0,10},{2,8},{4,14},{6,12},{8,2},{10,0},{12,6},{14,4},{1,11},{3,9}... | collective-permute-start | bytes 393224 | tf_op jit(solution)/shard_map/ppermute | solution.py:400
  12.1 14.8 %collective-permute-start.3 = (bf16[512,128]{1,0:T(8,128)(2,1)S(1)}, bf16[512,128]{1,0:T(8,128)(2,1)S(1)}, u32[]{:S(2)}, u32[]{:S(2)}) collective-permute-start(bf16[512,128]{1,0:T(8,128)(2,1)S(1)} %get-tuple-element.21.rest_0_), channel_id=1, source_target_pairs={{0,8},{2,10},{4,12},{6,14},{8,0},{10,2},{12,4},{14,6},{1,9},{3,11}... | collective-permute-start | bytes 393224 | tf_op jit(solution)/shard_map/ppermute | solution.py:400
  16.7 11.2 %collective-permute-start.5 = (bf16[512,128]{1,0:T(8,128)(2,1)S(1)}, bf16[512,128]{1,0:T(8,128)(2,1)S(1)}, u32[]{:S(2)}, u32[]{:S(2)}) collective-permute-start(bf16[512,128]{1,0:T(8,128)(2,1)S(1)} %get-tuple-element.26), channel_id=1, source_target_pairs={{0,2},{2,0},{4,6},{6,4},{8,10},{10,8},{12,14},{14,12},{1,3},{3,1},... | collective-permute-start | bytes 393224 | tf_op jit(solution)/shard_map/ppermute | solution.py:400
  17.1 13.1 %collective-permute-start.6 = (bf16[512,128]{1,0:T(8,128)(2,1)S(1)}, bf16[512,128]{1,0:T(8,128)(2,1)S(1)}, u32[]{:S(2)}, u32[]{:S(2)}) collective-permute-start(bf16[512,128]{1,0:T(8,128)(2,1)S(1)} %get-tuple-element.27), channel_id=1, source_target_pairs={{0,4},{2,6},{4,0},{6,2},{8,12},{10,14},{12,8},{14,10},{1,5},{3,7},... | collective-permute-start | bytes 393224 | tf_op jit(solution)/shard_map/ppermute | solution.py:400
  18.8 16.7 %collective-permute-start.7 = (bf16[512,128]{1,0:T(8,128)(2,1)S(1)}, bf16[512,128]{1,0:T(8,128)(2,1)S(1)}, u32[]{:S(2)}, u32[]{:S(2)}) collective-permute-start(bf16[512,128]{1,0:T(8,128)(2,1)S(1)} %get-tuple-element.28), channel_id=1, source_target_pairs={{0,6},{2,4},{4,2},{6,0},{8,14},{10,12},{12,10},{14,8},{1,7},{3,5},... | collective-permute-start | bytes 393224 | tf_op jit(solution)/shard_map/ppermute | solution.py:400
  20.2 15.3 %copy-start.3 = (f32[8,8]{1,0:T(8,128)S(1)}, f32[8,8]{1,0:T(8,128)}, u32[]{:S(2)}) copy-start(f32[8,8]{1,0:T(8,128)} %weights.5) | copy-start | bytes 772
  23.2 12.3 %collective-permute-start.1 = (bf16[512,128]{1,0:T(8,128)(2,1)S(1)}, bf16[512,128]{1,0:T(8,128)(2,1)S(1)}, u32[]{:S(2)}, u32[]{:S(2)}) collective-permute-start(bf16[512,128]{1,0:T(8,128)(2,1)S(1)} %get-tuple-element.23), channel_id=1, source_target_pairs={{0,12},{2,14},{4,8},{6,10},{8,4},{10,6},{12,0},{14,2},{1,13},{3,15... | collective-permute-start | bytes 393224 | tf_op jit(solution)/shard_map/ppermute | solution.py:400
  26.9 8.7 %collective-permute-start.2 = (bf16[512,128]{1,0:T(8,128)(2,1)S(1)}, bf16[512,128]{1,0:T(8,128)(2,1)S(1)}, u32[]{:S(2)}, u32[]{:S(2)}) collective-permute-start(bf16[512,128]{1,0:T(8,128)(2,1)S(1)} %get-tuple-element.24), channel_id=1, source_target_pairs={{0,14},{2,12},{4,10},{6,8},{8,6},{10,4},{12,2},{14,0},{1,15},{3,13... | collective-permute-start | bytes 393224 | tf_op jit(solution)/shard_map/ppermute | solution.py:400
  37.1 13.8 %collective-permute-start.12 = (bf16[512,128]{1,0:T(8,128)(2,1)S(1)}, bf16[512,128]{1,0:T(8,128)(2,1)S(1)}, u32[]{:S(2)}, u32[]{:S(2)}) collective-permute-start(bf16[512,128]{1,0:T(8,128)(2,1)S(1)} %get-tuple-element.33), channel_id=1, source_target_pairs={{0,8},{2,10},{4,12},{6,14},{8,0},{10,2},{12,4},{14,6},{1,9},{3,11}... | collective-permute-start | bytes 393224 | tf_op jit(solution)/shard_map/ppermute | solution.py:400
  39.9 15.2 %collective-permute-start.13 = (bf16[512,128]{1,0:T(8,128)(2,1)S(1)}, bf16[512,128]{1,0:T(8,128)(2,1)S(1)}, u32[]{:S(2)}, u32[]{:S(2)}) collective-permute-start(bf16[512,128]{1,0:T(8,128)(2,1)S(1)} %get-tuple-element.34), channel_id=1, source_target_pairs={{0,2},{2,0},{4,6},{6,4},{8,10},{10,8},{12,14},{14,12},{1,3},{3,1},... | collective-permute-start | bytes 393224 | tf_op jit(solution)/shard_map/ppermute | solution.py:400
  41.5 17.8 %collective-permute-start.8 = (bf16[512,128]{1,0:T(8,128)(2,1)S(1)}, bf16[512,128]{1,0:T(8,128)(2,1)S(1)}, u32[]{:S(2)}, u32[]{:S(2)}) collective-permute-start(bf16[512,128]{1,0:T(8,128)(2,1)S(1)} %get-tuple-element.29), channel_id=1, source_target_pairs={{0,10},{2,8},{4,14},{6,12},{8,2},{10,0},{12,6},{14,4},{1,11},{3,9}... | collective-permute-start | bytes 393224 | tf_op jit(solution)/shard_map/ppermute | solution.py:400
  41.5 13.6 %collective-permute-start.14 = (bf16[512,128]{1,0:T(8,128)(2,1)S(1)}, bf16[512,128]{1,0:T(8,128)(2,1)S(1)}, u32[]{:S(2)}, u32[]{:S(2)}) collective-permute-start(bf16[512,128]{1,0:T(8,128)(2,1)S(1)} %get-tuple-element.35), channel_id=1, source_target_pairs={{0,4},{2,6},{4,0},{6,2},{8,12},{10,14},{12,8},{14,10},{1,5},{3,7},... | collective-permute-start | bytes 393224 | tf_op jit(solution)/shard_map/ppermute | solution.py:400
  43.7 15.5 %collective-permute-start.9 = (bf16[512,128]{1,0:T(8,128)(2,1)S(1)}, bf16[512,128]{1,0:T(8,128)(2,1)S(1)}, u32[]{:S(2)}, u32[]{:S(2)}) collective-permute-start(bf16[512,128]{1,0:T(8,128)(2,1)S(1)} %get-tuple-element.30), channel_id=1, source_target_pairs={{0,12},{2,14},{4,8},{6,10},{8,4},{10,6},{12,0},{14,2},{1,13},{3,15... | collective-permute-start | bytes 393224 | tf_op jit(solution)/shard_map/ppermute | solution.py:400
  50.9 8.3 %collective-permute-start.10 = (bf16[512,128]{1,0:T(8,128)(2,1)S(1)}, bf16[512,128]{1,0:T(8,128)(2,1)S(1)}, u32[]{:S(2)}, u32[]{:S(2)}) collective-permute-start(bf16[512,128]{1,0:T(8,128)(2,1)S(1)} %get-tuple-element.31), channel_id=1, source_target_pairs={{0,14},{2,12},{4,10},{6,8},{8,6},{10,4},{12,2},{14,0},{1,15},{3,13... | collective-permute-start | bytes 393224 | tf_op jit(solution)/shard_map/ppermute | solution.py:400
  55.1 6.4 %collective-permute-start.11 = (bf16[512,128]{1,0:T(8,128)(2,1)S(1)}, bf16[512,128]{1,0:T(8,128)(2,1)S(1)}, u32[]{:S(2)}, u32[]{:S(2)}) collective-permute-start(bf16[512,128]{1,0:T(8,128)(2,1)S(1)} %get-tuple-element.32), channel_id=1, source_target_pairs={{0,6},{2,4},{4,2},{6,0},{8,14},{10,12},{12,10},{14,8},{1,7},{3,5},... | collective-permute-start | bytes 393224 | tf_op jit(solution)/shard_map/ppermute | solution.py:400
